TPU v7x, 256 devices: a whole 4x4x8 slice. The times are simulated.
256 devices in a mesh: ctx: 32 (over y, z), tp: 8 (over x, core).
Axes of the slice: x: 4, y: 4, z: 8, core: 2. Of those that a mesh axis runs over, the one named last changes fastest.
Arguments:
- context_queries: bfloat16 [24576, 8192], P('ctx', 'tp'), may hold values from -9 to 9
- context_keys: bfloat16 [24576, 1024], P('ctx', 'tp'), may hold values from -4 to 4
- context_value_rows: bfloat16 [24576, 1024], P('ctx', 'tp'), may hold values from -6 to 6
- prompt_queries: bfloat16 [512, 8192], P('ctx', 'tp'), may hold values from -9 to 9
- prompt_key_rows: bfloat16 [512, 1024], P('ctx', 'tp'), may hold values from -4 to 4
- prompt_value_matrix: bfloat16 [512, 1024], P('ctx', 'tp'), may hold values from -6 to 6
- output_weight: bfloat16 [8192, 8192], P('tp', 'ctx'), may hold values from -0.0625 to 0.0625
Outputs:
- encoded: bfloat16 [24576, 8192], P('ctx', 'tp')
- answered: bfloat16 [512, 8192], P('tp', 'ctx')
All inputs are finite; a program needn't handle non-finite values.
Results may differ from a plain program's by a relative error of at most 0.0049.
Values may be sent and summed in bfloat16 or wider, within the bound.
A program may use at most 64 MiB of HBM per device.

v0:
```python
import jax
import jax.numpy as jnp
from jax import lax
from jax.sharding import PartitionSpec as P

QUERY_HEADS = 64
KEY_VALUE_HEADS = 8
HEAD_SIZE = 128


def from_root(shard, axis, root):
    mine = lax.axis_index(axis) == root
    return lax.psum(jnp.where(mine, shard, jnp.zeros_like(shard)), axis)


def head_partial(query_rows, key_rows, value_rows, visible):
    scores = jnp.dot(query_rows, key_rows.T, preferred_element_type=jnp.float32) * HEAD_SIZE ** (
        -0.5
    )
    scores = jnp.where(visible, scores, -1e30)
    row_max = jnp.max(scores, axis=1)
    weights = jnp.exp(scores - row_max[:, None])
    row_sum = jnp.sum(weights, axis=1)
    accumulated = jnp.dot(
        weights.astype(jnp.bfloat16), value_rows, preferred_element_type=jnp.float32
    )
    return (row_max, row_sum, accumulated)


def columns(array, index):
    return lax.dynamic_slice_in_dim(array, index * HEAD_SIZE, HEAD_SIZE, 1)


def on_device(
    context_queries,
    context_keys,
    context_value_rows,
    prompt_queries,
    prompt_key_rows,
    prompt_value_matrix,
    output_weight,
):
    block_len = context_queries.shape[0]
    head_count = context_queries.shape[1] // HEAD_SIZE
    query_group_width = QUERY_HEADS // KEY_VALUE_HEADS
    anchor_keys, anchor_values = (
        from_root(context_keys, "ctx", 0),
        from_root(context_value_rows, "ctx", 0),
    )
    anchored = lax.axis_index("ctx") > 0
    positions = jnp.arange(block_len, dtype=jnp.int32)
    causal = positions[None, :] <= positions[:, None]
    key_block = jnp.concatenate([anchor_keys, context_keys], axis=0)
    value_block = jnp.concatenate([anchor_values, context_value_rows], axis=0)
    visible = jnp.concatenate([jnp.broadcast_to(anchored, (block_len, block_len)), causal], axis=1)

    def encode_head(head_index):
        kv_head = head_index // query_group_width
        row_max, row_sum, accumulated = head_partial(
            columns(context_queries, head_index),
            columns(key_block, kv_head),
            columns(value_block, kv_head),
            visible,
        )
        return (accumulated / row_sum[:, None]).astype(jnp.bfloat16)

    per_head = lax.map(encode_head, jnp.arange(head_count, dtype=jnp.int32))
    encoded = jnp.transpose(per_head, (1, 0, 2)).reshape(block_len, head_count * HEAD_SIZE)
    gathered = lax.all_gather(prompt_queries, "ctx", axis=0, tiled=True)
    query_total = gathered.shape[0]
    share_rows = prompt_key_rows.shape[0]
    own_rows = lax.axis_index("ctx") * share_rows + jnp.arange(share_rows, dtype=jnp.int32)
    query_positions = jnp.arange(query_total, dtype=jnp.int32)
    prompt_key_block = jnp.concatenate([context_keys, prompt_key_rows], axis=0)
    prompt_value_block = jnp.concatenate([context_value_rows, prompt_value_matrix], axis=0)
    prompt_visible = jnp.concatenate(
        [
            jnp.ones((query_total, block_len), dtype=jnp.bool_),
            own_rows[None, :] <= query_positions[:, None],
        ],
        axis=1,
    )

    def prompt_head(head_index):
        kv_head = head_index // query_group_width
        return head_partial(
            columns(gathered, head_index),
            columns(prompt_key_block, kv_head),
            columns(prompt_value_block, kv_head),
            prompt_visible,
        )

    row_max, row_sum, accumulated = lax.map(prompt_head, jnp.arange(head_count, dtype=jnp.int32))
    overall = lax.pmax(row_max, "ctx")
    factor = jnp.exp(row_max - overall)
    numerator, denominator = lax.psum((accumulated * factor[..., None], row_sum * factor), "ctx")
    attended = (numerator / denominator[..., None]).astype(jnp.bfloat16)
    attended = jnp.transpose(attended, (1, 0, 2)).reshape(query_total, head_count * HEAD_SIZE)
    answered = lax.psum_scatter(
        jnp.dot(attended, output_weight, preferred_element_type=jnp.float32),
        "tp",
        scatter_dimension=0,
        tiled=True,
    ).astype(jnp.bfloat16)
    return (encoded, answered)


def solution(mesh):
    placed = (
        P("ctx", "tp"),
        P("ctx", "tp"),
        P("ctx", "tp"),
        P("ctx", "tp"),
        P("ctx", "tp"),
        P("ctx", "tp"),
        P("tp", "ctx"),
    )
    return jax.shard_map(
        on_device,
        mesh=mesh,
        in_specs=placed,
        out_specs=(P("ctx", "tp"), P("tp", "ctx")),
        check_vma=False,
    )
```

profile of v0, /device:TPU:17, one launch (start us, length us, event | category | flops | bytes accessed | tf_op | source)
XLA Modules:
  0.0 468.7 jit_solution(5349295606758950484)
XLA Ops:
  10.1 73.6 %all-gather.2.cloned.1.call-done = bf16[512,1024]{1,0:T(8,128)(2,1)} async-done(((bf16[16,1024]{1,0:T(8,128)(2,1)}), bf16[512,1024]{1,0:T(8,128)(2,1)}) %all-gather.2.cloned.1.call-update) | async-done | bytes 1048592 | tf_op jit(solution)/shard_map/all_gather | solution.py:69
  83.7 34.1 %while.25 = (s32[]{:T(128)}, f32[8,512]{1,0:T(8,128)S(1)}, f32[8,512]{1,0:T(8,128)S(1)}, f32[8,512,128]{1,2,0:T(8,128)}, s32[8]{0:T(128)S(1)}, /*index=5*/bf16[5...) while((s32[]{:T(128)}, f32[8,512]{1,0:T(8,128)S(1)}, ...), condition=%wide.region_9.10_spmd, body=%wide.region_6.9_spmd.sunk | while | flops 208329728 | bytes 6029519 | solution.py:93
  117.8 93.2 %pmax.7 = f32[8,512]{1,0:T(8,128)S(1)} all-reduce(f32[8,512]{1,0:T(8,128)S(1)} %get-tuple-element.90), channel_id=1, replica_groups=mesh['ctx'=32,'tp'=8] {'ctx'}, use_global_device_ids=true, to_apply=%region_10.11 | all-reduce | flops 4096 | bytes 32768 | tf_op jit(solution)/shard_map/pmax | solution.py:94
  211.1 3.3 broadcast_multiply_fusion
  215.3 15.6 %all-reduce.8.cloned.1.call-done = (bf16[768,128]{1,0:T(8,128)(2,1)}, bf16[768,128]{1,0:T(8,128)(2,1)}) async-done(((bf16[768,128]{1,0:T(8,128)(2,1)}, bf16[768,128]{1,0:T(8,128)(2,1)}), (bf16[768,128]{1,0:T(8,128)(2,1)}, bf16[768,128]{1,0:T(8,128)(2,1)})) %all-reduce.8.cloned.1.call-update) | async-done | bytes 393232 | tf_op jit(solution)/shard_map/psum | solution.py:13
  232.8 93.9 %psum.31 = f32[8,512]{1,0:T(8,128)S(1)} all-reduce(f32[8,512]{1,0:T(8,128)S(1)} %get-tuple-element.126), channel_id=1, replica_groups=mesh['ctx'=32,'tp'=8] {'ctx'}, use_global_device_ids=true, to_apply=%region_12.13 | all-reduce | flops 4096 | bytes 32768 | tf_op jit(solution)/shard_map/psum | solution.py:96
  326.7 83.2 %all-reduce.6.cloned.1.call-done = f32[8,512,128]{1,2,0:T(8,128)} async-done(((f32[8,512,128]{1,2,0:T(8,128)}), f32[8,512,128]{1,2,0:T(8,128)}) %all-reduce.6.cloned.1.call-update) | async-done | bytes 2097168 | tf_op jit(solution)/shard_map/psum | solution.py:96
  410.0 1.9 divide_convert_fusion
  413.1 44.8 %while.24 = (s32[]{:T(128)}, bf16[8,768,128]{2,1,0:T(8,128)(2,1)}, s32[8]{0:T(128)S(1)}, bf16[768,1024]{1,0:T(8,128)(2,1)}, bf16[1536,128]{1,0:T(8,128)(2,1)S(1)...) while((s32[]{:T(128)}, bf16[8,768,128]{2,1,0:T(8,128)(2,1)}, ...), condition=%wide.region_5.6_spmd, body=%wide.region_2.5_spmd.sunk | while | flops 612432384 | bytes 16530615 | solution.py:67
  414.4 2.0 fusion.52
  417.2 1.6 fusion.54
  420.0 2.0 fusion.52
  425.6 2.0 fusion.52
  428.4 1.6 fusion.54
  431.2 2.0 fusion.52
  434.0 1.6 fusion.54
  436.8 2.0 fusion.52
  439.6 1.6 fusion.54
  442.4 2.0 fusion.52
  445.2 1.6 fusion.54
  448.0 2.0 fusion.52
  453.6 2.0 fusion.52
  456.3 1.6 fusion.54
  457.9 2.8 copy_bitcast_fusion
  (100 shorter events, 50.7 us)
Async XLA Ops:
  7.2 404.7 %copy-start = (bf16[1024,256]{1,0:T(8,128)(2,1)S(1)}, bf16[1024,256]{1,0:T(8,128)(2,1)}, u32[]{:S(2)}) copy-start(bf16[1024,256]{1,0:T(8,128)(2,1)} %param.17) | copy-start | bytes 1572868
  7.2 76.6 %all-gather.2.cloned.1.call-start = ((), (), s32[]{:S(2)}) async-start(), calls=%async_computation.1 | async-start | bytes 1081344 | tf_op jit(solution)/shard_map/all_gather | solution.py:69
  7.9 223.0 %all-reduce.8.cloned.1.call-start = ((), (), s32[]{:S(2)}) async-start(), calls=%async_computation.4 | async-start | bytes 786432 | tf_op jit(solution)/shard_map/psum | solution.py:13
  8.8 401.2 %all-reduce.6.cloned.1.call-start = ((), (), s32[]{:S(2)}) async-start(), calls=%async_computation.2 | async-start | bytes 4194304 | tf_op jit(solution)/shard_map/psum | solution.py:96
  214.4 246.3 %reduce-scatter.2.cloned.1.call-start = ((), (), s32[]{:S(2)}) async-start(), calls=%async_computation.3 | async-start | bytes 589824 | tf_op jit(solution)/shard_map/reduce_scatter | solution.py:99
  214.8 16.1 %copy-start.1 = (bf16[768,128]{1,0:T(8,128)(2,1)S(1)}, bf16[768,128]{1,0:T(8,128)(2,1)}, u32[]{:S(2)}) copy-start(bf16[768,128]{1,0:T(8,128)(2,1)} %param.12) | copy-start | bytes 589828
  214.9 17.0 %copy-start.2 = (bf16[768,128]{1,0:T(8,128)(2,1)S(1)}, bf16[768,128]{1,0:T(8,128)(2,1)}, u32[]{:S(2)}) copy-start(bf16[768,128]{1,0:T(8,128)(2,1)} %param.13) | copy-start | bytes 589828
Sparse Core Ops, SparseCore 0:
  10.6 73.0 all-gather.1
  87.8 143.0 all-reduce.7
  234.8 175.0 all-reduce.5
  413.3 33.1 reduce-scatter.1
where the time goes:
time: 475 us; the launch traced here: 469 us
  blocking collectives  187 us (39%)
  waiting for transfers between devices  173 us (36%)
  matrix products  49.8 us (10%)
  other arithmetic  19.1 us (4%)
  local copies, waits for them, and re-layouts  14.4 us (3%)
  between operations  13.9 us (3%)
  loops' own time  11.1 us (2%)
    psum x1, blocking collectives, on_device(): lax.psum((accumulated * factor[..., None], row_sum * factor), 'ctx')  93.9 us
    pmax x1, blocking collectives, on_device(): overall = lax.pmax(row_max, 'ctx')  93.2 us
    psum x1, waiting for transfers between devices, on_device(): lax.psum((accumulated * factor[..., None], row_sum * factor), 'ctx')  83.2 us
    all_gather x1, waiting for transfers between devices, on_device(): gathered = lax.all_gather(prompt_queries, 'ctx', axis=0, tiled=True)  73.6 us
    dot_general x16, matrix products, head_partial(): jnp.dot(query_rows, key_rows.T, preferred_element_type=jnp.float32)  26.8 us
    dot_general x16, matrix products, head_partial(): jnp.dot(weights.astype(jnp.bfloat16), value_rows, preferred_element_type=...  21.8 us
    psum x1, waiting for transfers between devices, from_root(): return lax.psum(jnp.where(mine, shard, jnp.zeros_like(shard)), axis)  15.6 us
    dynamic_slice x16, local copies, waits for them, and re-layouts, on_device(): per_head = lax.map(encode_head, jnp.arange(head_count, dtype=jnp.int32))  9.94 us
  transfers between devices with their start and end apart: 4, of which 3 were waited for; matrix products, arithmetic and copies ran while one was open for 17% of the time, Pallas kernels for 0%

commit v1 on v0

v1 whole, which is shorter than its diff:
```python
import functools

import jax
import jax.numpy as jnp
from jax import lax
from jax.experimental import pallas as pl
from jax.experimental.pallas import tpu as pltpu
from jax.sharding import PartitionSpec as P

MESH = pl.DeviceIdType.MESH
F32 = jnp.float32
BF16 = jnp.bfloat16
HEAD = 128
HEADS = 8
NY, NZ, NT = 4, 8, 8
BLK = 768
ROWS = 16
WIDE = HEADS * HEAD
MSG = WIDE + 128
KEYS = BLK + 128
PIECE = 2 * BLK // NZ
UNIT = 384
C2 = HEAD**-0.5 * 1.4426950408889634
NEG = -1e30


def dot(a, b):
    return jnp.dot(a, b, preferred_element_type=F32)


def kernel(
    cq, ck, cv, pq, pk, pv, w,
    enc, ans,
    q_v, k_v, v_v, pk_v, pv_v, w_v,
    kt, va, kta, vaa,
    om, out_v,
    qall, att, anc,
    po, ps, r1s, r1d, r2s, r2d, r3s, r3d,
    tsend, tgot, town,
    loc, q_zs, q_fs, q_rs, q_rr,
    a_zs, a_fs, a_rs, a_rr,
    n_ss, n_ys, n_zs, n_rr,
    r1_ss, r1_rr, r2_ss, r2_rr, r3_ss, r3_rr,
    t_ss, t_rr,
):
    c = lax.axis_index("ctx")
    t = lax.axis_index("tp")
    y, z = c // NZ, c % NZ
    up, down = (y + 1) % NY, (y + NY - 1) % NY

    def remote(src, dst, ss, rr, dev):
        return pltpu.make_async_remote_copy(
            src_ref=src, dst_ref=dst, send_sem=ss, recv_sem=rr,
            device_id=dev, device_id_type=MESH,
        )

    def arrived(ref, sem):
        pltpu.make_async_copy(ref, ref, sem).wait()

    local = [
        pltpu.make_async_copy(pq, qall.at[c], loc.at[0]),
        pltpu.make_async_copy(ck, k_v, loc.at[1]),
        pltpu.make_async_copy(cv, v_v, loc.at[2]),
        pltpu.make_async_copy(cq, q_v, loc.at[3]),
        pltpu.make_async_copy(pk, pk_v, loc.at[4]),
        pltpu.make_async_copy(pv, pv_v, loc.at[5]),
        pltpu.make_async_copy(w, w_v, loc.at[6]),
    ]
    for copy in local:
        copy.start()

    barrier = pltpu.get_barrier_semaphore()
    for d in range(1, NZ):
        pl.semaphore_signal(barrier, inc=1, device_id=(y * NZ + (z + d) % NZ, t), device_id_type=MESH)
    for row in (up, down):
        pl.semaphore_signal(barrier, inc=1, device_id=(row * NZ + z, t), device_id_type=MESH)
    for d in range(1, NT):
        pl.semaphore_signal(barrier, inc=1, device_id=(c, (t + d) % NT), device_id_type=MESH)
    pl.semaphore_wait(barrier, NZ - 1 + 2 + NT - 1)

    def zed(j):
        return (z + jnp.where(j % 2 == 1, (j + 1) // 2, NZ - j // 2)) % NZ

    class Gather:
        def __init__(self, buf, zs, fs, rs, rr):
            self.buf, self.zs, self.fs, self.rs, self.rr = buf, zs, fs, rs, rr

        def zsend(self, d):
            return remote(self.buf.at[c], self.buf.at[c], self.zs.at[d], self.rr.at[c],
                          (y * NZ + (z + d) % NZ, t))

        def forward(self, j, way):
            s = y * NZ + zed(j)
            row = up if way == 0 else down
            return remote(self.buf.at[s], self.buf.at[s], self.fs.at[way, j], self.rr.at[s],
                          (row * NZ + z, t))

        def passing(self, j):
            upward = 1 - j % 2
            s = ((y + 1 + 2 * upward) % NY) * NZ + zed(j)
            row = (y + 3 - 2 * upward) % NY
            return remote(self.buf.at[s], self.buf.at[s], self.rs.at[j], self.rr.at[s],
                          (row * NZ + z, t))

        def wait(self, s):
            arrived(self.buf.at[s], self.rr.at[s])

        def start(self):
            for d in (1, 7, 2, 6, 3, 5, 4):
                self.zsend(d).start()

        def step(self, j):
            @pl.when(j > 0)
            def _():
                self.wait(y * NZ + zed(j))

            self.forward(j, 0).start()
            self.forward(j, 1).start()

        def relay(self, j):
            self.wait(down * NZ + zed(j))
            self.wait(up * NZ + zed(j))
            self.passing(j).start()

        def drain(self):
            for d in range(1, NZ):
                self.zsend(d).wait_send()

            def one(j, carry):
                self.forward(j, 0).wait_send()
                self.forward(j, 1).wait_send()
                self.passing(j).wait_send()
                return carry

            lax.fori_loop(0, NZ, one, 0)

    queries = Gather(qall, q_zs, q_fs, q_rs, q_rr)
    attended = Gather(att, a_zs, a_fs, a_rs, a_rr)

    local[0].wait()
    queries.start()

    def root_send(p):
        if p < NZ // 2:
            src = ck.at[pl.ds(p * PIECE, PIECE)]
        else:
            src = cv.at[pl.ds((p - NZ // 2) * PIECE, PIECE)]
        return remote(src, anc.at[p], n_ss.at[p], n_rr.at[p], (p, t))

    def anchor_y(row, i):
        return remote(anc.at[z], anc.at[z], n_ys.at[i], n_rr.at[z], (row * NZ + z, t))

    def anchor_z(d):
        return remote(anc.at[z], anc.at[z], n_zs.at[d], n_rr.at[z], (y * NZ + (z + d) % NZ, t))

    root_own = pltpu.make_async_copy(ck.at[pl.ds(0, PIECE)], anc.at[0], loc.at[7])

    @pl.when(c == 0)
    def _():
        root_own.start()
        for p in (1, 7, 2, 6, 3, 5, 4):
            root_send(p).start()

    def anchor_step():
        @pl.when(c == 0)
        def _():
            root_own.wait()

        @pl.when(c != 0)
        def _():
            arrived(anc.at[z], n_rr.at[z])

        @pl.when(y == 0)
        def _():
            anchor_y(1, 0).start()
            anchor_y(3, 1).start()

        @pl.when(y == 1)
        def _():
            anchor_y(2, 0).start()

        for d in (1, 7, 2, 6, 3, 5, 4):
            anchor_z(d).start()

    for copy in local[1:]:
        copy.wait()

    kt[:, :BLK] = k_v[...].T
    kt[:, BLK:] = jnp.concatenate([pk_v[...], jnp.zeros((128 - ROWS, HEAD), BF16)], axis=0).T
    va[:BLK, :HEAD] = v_v[...]
    va[BLK : BLK + ROWS, :HEAD] = pv_v[...]
    va[BLK + ROWS :, :HEAD] = jnp.zeros((128 - ROWS, HEAD), BF16)
    va[:, HEAD:] = jnp.ones((KEYS, HEAD), BF16)

    def own_head(h):
        cols = pl.ds(pl.multiple_of(h * HEAD, HEAD), HEAD)
        r = 256
        row = lax.broadcasted_iota(jnp.int32, (r, r), 0)
        col = lax.broadcasted_iota(jnp.int32, (r, r), 1)
        tiles = range(BLK // r)
        scores = []
        for i in tiles:
            s = dot(q_v[r * i : r * (i + 1), cols], kt[:, : r * (i + 1)])
            last = jnp.where(col <= row, s[:, r * i :], NEG)
            scores.append(jnp.concatenate([s[:, : r * i], last], axis=1) if i else last)
        maxima = [jnp.max(s, axis=1, keepdims=True) for s in scores]
        weights = [jnp.exp2(s * C2 - m * C2).astype(BF16) for s, m in zip(scores, maxima)]
        for i in tiles:
            om[h, r * i : r * (i + 1), : 2 * HEAD] = dot(weights[i], va[: r * (i + 1)])
            om[h, r * i : r * (i + 1), 2 * HEAD :] = jnp.broadcast_to(maxima[i], (r, HEAD))

    def loop_a(j, carry):
        queries.step(j)

        @pl.when(j > 0)
        def _():
            queries.relay(j - 1)

        @pl.when(((j == 4) & (y == 0)) | ((j == 6) & (y % 2 == 1)))
        def _():
            anchor_step()

        own_head(j)
        return carry

    lax.fori_loop(0, NZ, loop_a, 0)
    queries.relay(NZ - 1)

    @pl.when(y == 2)
    def _():
        anchor_step()

    lane = lax.broadcasted_iota(jnp.int32, (ROWS, 128), 1)
    QUAD = 4

    def prompt(row, first):
        blocks = []
        for g in range(QUAD):
            s = row * NZ + zed(first + g)
            for h in range(HEADS):
                blocks.append(qall[s, :, HEAD * h : HEAD * (h + 1)])
        s = dot(jnp.concatenate(blocks, axis=0), kt[...])
        r = lax.broadcasted_iota(jnp.int32, (HEADS * ROWS, 128), 0) % ROWS
        k = lax.broadcasted_iota(jnp.int32, (HEADS * ROWS, 128), 1)
        last = []
        for g in range(QUAD):
            ahead = (row * NZ + zed(first + g) - c) * ROWS
            tile = s[HEADS * ROWS * g : HEADS * ROWS * (g + 1), BLK:]
            last.append(jnp.where((k < ROWS) & (k <= r + ahead), tile, NEG))
        s = jnp.concatenate([s[:, :BLK], jnp.concatenate(last, axis=0)], axis=1)
        m = jnp.ceil(jnp.max(s, axis=1, keepdims=True) * (C2 / 4)) * 4
        o = dot(jnp.exp2(s * C2 - m).astype(BF16), va[...])
        for g in range(QUAD):
            stats = jnp.zeros((ROWS, 128), F32)
            for h in range(HEADS):
                at = (g * HEADS + h) * ROWS
                po[g, :, HEAD * h : HEAD * (h + 1)] = o[at : at + ROWS, :HEAD]
                stats = jnp.where(lane == h, o[at : at + ROWS, HEAD:], stats)
                stats = jnp.where(lane == 16 + h, m[at : at + ROWS], stats)
            ps[g] = stats

    def split(stats):
        high = stats.astype(BF16).astype(F32)
        rest = pltpu.roll(stats - high, 8, 1)
        return jnp.where((lane >= 8) & (lane < 16), rest, high).astype(BF16)

    def put(dst, g):
        dst[:, :WIDE] = po[g].astype(BF16)
        dst[:, WIDE:] = split(ps[g])

    def whole(stats):
        return jnp.where(lane < 8, stats + pltpu.roll(stats, 120, 1), stats)

    def merge(parts):
        top = functools.reduce(jnp.maximum, [stats for _, stats in parts])
        factors = [jnp.exp2(stats - top) for _, stats in parts]
        total = sum(stats * pltpu.roll(f, 112, 1) for (_, stats), f in zip(parts, factors))
        stats = jnp.where(lane < 8, total, jnp.where((lane >= 16) & (lane < 24), top, 0.0))
        results = []
        for h in range(HEADS):
            cols = slice(HEAD * h, HEAD * (h + 1))
            results.append(sum(
                read(cols) * f[:, 16 + h : 17 + h] for (read, _), f in zip(parts, factors)
            ))
        return results, stats

    def mine(g):
        return (lambda cols: po[g, :, cols]), ps[g]

    def got(ref):
        return (lambda cols: ref[:, cols].astype(F32)), whole(ref[:, WIDE:].astype(F32))

    def put_merged(dst, parts):
        results, stats = merge(parts)
        for h in range(HEADS):
            dst[:, HEAD * h : HEAD * (h + 1)] = results[h].astype(BF16)
        dst[:, WIDE:] = split(stats)

    def send1(j):
        row = (y + 1 + 2 * (j % 2)) % NY
        return remote(r1s.at[j], r1d.at[j], r1_ss.at[j], r1_rr.at[j], (row * NZ + z, t))

    def send2(way, j):
        row = up if way == 0 else down
        return remote(r2s.at[way, j], r2d.at[way, j], r2_ss.at[way, j], r2_rr.at[way, j], (row * NZ + z, t))

    def send3(j):
        return remote(r3s.at[j], r3d.at[j], r3_ss.at[j], r3_rr.at[j], (y * NZ + zed(j), t))

    def phase1(b, carry):
        far = (y + 2) % NY
        for g in range(QUAD):
            queries.wait(far * NZ + zed(b * QUAD + g))
        prompt(far, b * QUAD)
        for g in range(QUAD):
            put(r1s.at[b * QUAD + g], g)
            send1(b * QUAD + g).start()
        return carry

    lax.fori_loop(0, NZ // QUAD, phase1, 0)

    def phase2(b, carry):
        for way, row in ((0, up), (1, down)):
            prompt(row, b * QUAD)
            for g in range(QUAD):
                j = b * QUAD + g
                if g % 2 == way:
                    arrived(r1d.at[j], r1_rr.at[j])
                    put_merged(r2s.at[way, j], [mine(g), got(r1d.at[j])])
                else:
                    put(r2s.at[way, j], g)
                send2(way, j).start()
        return carry

    lax.fori_loop(0, NZ // QUAD, phase2, 0)

    def anchor_ready():
        for p in range(NZ):
            @pl.when(z != p)
            def _(p=p):
                arrived(anc.at[p], n_rr.at[p])
        for p in range(NZ // 2):
            kta[:, PIECE * p : PIECE * (p + 1)] = anc[p].T
            vaa[PIECE * p : PIECE * (p + 1), :HEAD] = anc[NZ // 2 + p]
        vaa[:, HEAD:] = jnp.ones((BLK, HEAD), BF16)

    seen = jnp.where(c > 0, 0.0, NEG)

    def anchor_unit(u, carry):
        h, i = u // (BLK // UNIT), u % (BLK // UNIT)
        cols = pl.ds(pl.multiple_of(h * HEAD, HEAD), HEAD)
        rows = pl.ds(pl.multiple_of(i * UNIT, UNIT), UNIT)
        s = dot(q_v[rows, cols], kta[...])
        m = jnp.max(s, axis=1, keepdims=True)
        o = dot(jnp.exp2(s * C2 - m * C2).astype(BF16), vaa[...])
        m = m + seen
        own = om[h, rows, 2 * HEAD :]
        top = jnp.maximum(m, own)
        f_own, f = jnp.exp2((own - top) * C2), jnp.exp2((m - top) * C2)
        above = om[h, rows, :HEAD] * f_own + o[:, :HEAD] * f
        below = om[h, rows, HEAD : 2 * HEAD] * f_own + o[:, HEAD:] * f
        out_v[rows, cols] = (above / below).astype(BF16)
        return carry

    UNITS = HEADS * (BLK // UNIT)

    def phase3(b):
        prompt(y, b * QUAD)
        for g in range(QUAD):
            j = b * QUAD + g
            for way in (0, 1):
                arrived(r2d.at[way, j], r2_rr.at[way, j])
            put_merged(r3s.at[j], [mine(g), got(r2d.at[0, j]), got(r2d.at[1, j])])
            if j:
                send3(j).start()

    phase3(0)
    anchor_ready()
    lax.fori_loop(0, 2, anchor_unit, 0)
    phase3(1)
    lax.fori_loop(2, UNITS - NZ, anchor_unit, 0)

    for j in range(1, NZ):
        arrived(r3d.at[j], r3_rr.at[j])
    results, stats = merge([got(r3s.at[0])] + [got(r3d.at[j]) for j in range(1, NZ)])
    for h in range(HEADS):
        att[c, :, HEAD * h : HEAD * (h + 1)] = (results[h] / stats[:, h : h + 1]).astype(BF16)

    attended.start()

    def loop_b(j, carry):
        attended.step(j)

        @pl.when(j > 0)
        def _():
            attended.relay(j - 1)

        anchor_unit(UNITS - NZ + j, carry)
        return carry

    lax.fori_loop(0, NZ, loop_b, 0)
    attended.relay(NZ - 1)
    enc_out = pltpu.make_async_copy(out_v, enc, loc.at[8])
    enc_out.start()

    half = 2 * NZ * ROWS // 4

    def tp_send(to):
        return remote(tsend.at[to], tgot.at[t], t_ss.at[to], t_rr.at[t], (c, to))

    for g in (0, 1, 3, 2):
        row = (y + g) % NY
        if g == 2:
            for j in range(NZ):
                attended.wait(row * NZ + zed(j))
        a = jnp.concatenate([att[row * NZ + i] for i in range(NZ)], axis=0)
        part = dot(a, w_v[...])
        for b in range(2):
            to = 2 * row + b
            piece = part[half * b : half * (b + 1)]

            @pl.when(to == t)
            def _(piece=piece):
                town[...] = piece

            @pl.when(to != t)
            def _(piece=piece, to=to):
                tsend[to] = piece.astype(BF16)
                tp_send(to).start()

    for d in range(1, NT):
        other = (t + d) % NT
        arrived(tgot.at[other], t_rr.at[other])
    ans[...] = (town[...] + sum(tgot[(t + d) % NT].astype(F32) for d in range(1, NT))).astype(BF16)

    queries.drain()
    attended.drain()
    for d in range(1, NZ):
        anchor_z(d).wait_send()

    @pl.when(c == 0)
    def _():
        for p in range(1, NZ):
            root_send(p).wait_send()

    @pl.when(y == 0)
    def _():
        anchor_y(1, 0).wait_send()
        anchor_y(3, 1).wait_send()

    @pl.when(y == 1)
    def _():
        anchor_y(2, 0).wait_send()

    for j in range(NZ):
        send1(j).wait_send()
        send2(0, j).wait_send()
        send2(1, j).wait_send()
        if j:
            send3(j).wait_send()
    for d in range(1, NT):
        tp_send((t + d) % NT).wait_send()
    enc_out.wait()


def on_device(cq, ck, cv, pq, pk, pv, w):
    vm, dma = pltpu.VMEM, pltpu.SemaphoreType.DMA
    feats = w.shape[1]
    half = 2 * NZ * ROWS // 4
    any_space = pl.BlockSpec(memory_space=pl.ANY)
    return pl.pallas_call(
        kernel,
        out_shape=(
            jax.ShapeDtypeStruct((BLK, WIDE), BF16),
            jax.ShapeDtypeStruct((half, feats), BF16),
        ),
        in_specs=[any_space] * 7,
        out_specs=(any_space, pl.BlockSpec(memory_space=pltpu.VMEM)),
        scratch_shapes=[
            vm((BLK, WIDE), BF16), vm((BLK, HEAD), BF16), vm((BLK, HEAD), BF16),
            vm((ROWS, HEAD), BF16), vm((ROWS, HEAD), BF16), vm((WIDE, feats), BF16),
            vm((HEAD, KEYS), BF16), vm((KEYS, 2 * HEAD), BF16),
            vm((HEAD, BLK), BF16), vm((BLK, 2 * HEAD), BF16),
            vm((HEADS, BLK, 3 * HEAD), F32), vm((BLK, WIDE), BF16),
            vm((NY * NZ, ROWS, WIDE), BF16), vm((NY * NZ, ROWS, WIDE), BF16),
            vm((NZ, PIECE, HEAD), BF16),
            vm((4, ROWS, WIDE), F32), vm((4, ROWS, 128), F32),
            vm((NZ, ROWS, MSG), BF16), vm((NZ, ROWS, MSG), BF16),
            vm((2, NZ, ROWS, MSG), BF16), vm((2, NZ, ROWS, MSG), BF16),
            vm((NZ, ROWS, MSG), BF16), vm((NZ, ROWS, MSG), BF16),
            vm((NT, half, feats), BF16), vm((NT, half, feats), BF16), vm((half, feats), F32),
            dma((9,)), dma((NZ,)), dma((2, NZ)), dma((NZ,)), dma((NY * NZ,)),
            dma((NZ,)), dma((2, NZ)), dma((NZ,)), dma((NY * NZ,)),
            dma((NZ,)), dma((2,)), dma((NZ,)), dma((NZ,)),
            dma((NZ,)), dma((NZ,)), dma((2, NZ)), dma((2, NZ)), dma((NZ,)), dma((NZ,)),
            dma((NT,)), dma((NT,)),
        ],
        compiler_params=pltpu.CompilerParams(
            collective_id=0, has_side_effects=True, vmem_limit_bytes=56 * 2**20
        ),
        cost_estimate=pl.CostEstimate(flops=12 * 10**9, bytes_accessed=5 * 10**6, transcendentals=11 * 10**6),
        name="star",
    )(cq, ck, cv, pq, pk, pv, w)


def solution(mesh):
    placed = (P("ctx", "tp"),) * 6 + (P("tp", "ctx"),)
    return jax.shard_map(
        on_device,
        mesh=mesh,
        in_specs=placed,
        out_specs=(P("ctx", "tp"), P("tp", "ctx")),
        check_vma=False,
    )
```

time: 475 us -> 91.9 us (0.19); the launches traced: 469 us -> 91.8 us
  blocking collectives: 187 us -> 0 us
  waiting for transfers between devices: 173 us -> 0 us
  Pallas kernels: 0 us -> 87.8 us
  matrix products: 49.8 us -> 0 us
  other arithmetic: 19.1 us -> 0 us
  between operations: 13.9 us -> 0.65 us
  local copies, waits for them, and re-layouts: 14.4 us -> 3.29 us
  loops' own time: 11.1 us -> 0 us
    psum x2 -> x0, waiting for transfers between devices: 98.9 us -> none  [the longest x1 83.2 us: on_device(): lax.psum((accumulated * factor[..., None], row_sum * factor), 'ctx')]
    psum x1 -> x0, blocking collectives: 93.9 us -> none  [on_device(): lax.psum((accumulated * factor[..., None], row_sum * factor), 'ctx')]
    pmax x1 -> x0, blocking collectives: 93.2 us -> none  [on_device(): overall = lax.pmax(row_max, 'ctx')]
    pallas_call x0 -> x1, Pallas kernels: none -> 87.8 us  [on_device(): pl.pallas_call(kernel, out_shape=(jax.ShapeDtypeStruct((BLK, WIDE), BF16)...]
    all_gather x1 -> x0, waiting for transfers between devices: 73.6 us -> none  [on_device(): gathered = lax.all_gather(prompt_queries, 'ctx', axis=0, tiled=True)]
    dot_general x33 -> x0, matrix products: 49.8 us -> none  [the longest x16 26.8 us: head_partial(): jnp.dot(query_rows, key_rows.T, preferred_element_type=jnp.float32)]
    another operation x2 -> x0, loops' own time: 11.1 us -> none  [the longest x1 5.77 us: on_device(): lax.map(prompt_head, jnp.arange(head_count, dtype=jnp.int32))]
    dynamic_slice x16 -> x0, local copies, waits for them, and re-layouts: 9.94 us -> none  [on_device(): per_head = lax.map(encode_head, jnp.arange(head_count, dtype=jnp.int32))]
  transfers between devices with their start and end apart: 4 -> 0, of which waited for: 3 -> 0; matrix products, arithmetic and copies ran while one was open for 17% -> 0% of each run, Pallas kernels for 0% -> 0%
where the time goes in v1:
time: 91.9 us; the launch traced here: 91.8 us
  Pallas kernels  87.8 us (96%)
  local copies, waits for them, and re-layouts  3.29 us (4%)
    pallas_call x1, Pallas kernels, on_device(): pl.pallas_call(kernel, out_shape=(jax.ShapeDtypeStruct((BLK, WIDE), BF16)...  87.8 us
    unnamed x4, local copies, waits for them, and re-layouts  3.29 us

profile of v1, /device:TPU:17, one launch (start us, length us, event | category | flops | bytes accessed | tf_op | source)
XLA Modules:
  0.0 91.8 jit_solution(17479885359649763892)
XLA Ops:
  0.6 87.8 %star.1 = (bf16[768,1024]{1,0:T(8,128)(2,1)}, bf16[64,256]{1,0:T(8,128)(2,1)}) custom-call(bf16[768,1024]{1,0:T(8,128)(2,1)} %cq.1, bf16[768,128]{1,0:T(8,128)(2,1)} %ck.1, bf16[768,128]{1,0:T(8,128)(2,1)} %cv.1, bf16[16,1024]{1,0:T(8,128)(2,1)} %pq.1, bf16[16,128]{1,0:T(8,128)(2,1)} %pk.1, bf16[16,128]{1,0:T(8,128)(2,1)} %pv.1, bf16[1024,256]{1,0:T(8,128)(2,1)} %w.1), custom_call_target="tpu_custom_call" | custom-call | flops 12000000000 | bytes 5000000 | tf_op jit(solution)/shard_map/star/pallas_call | solution.py:471
  88.5 0.0 copy-start
  88.5 2.7 %copy.11 = bf16[768,1024]{1,0:T(8,128)(2,1)} copy(bf16[768,1024]{1,0:T(8,128)(2,1)} %get-tuple-element.4) | data formatting | bytes 3145728
  91.2 0.0 copy-done
  91.2 0.6 copy.12
Async XLA Ops:
  88.5 2.7 %copy-start = (bf16[64,256]{1,0:T(8,128)(2,1)S(1)}, bf16[64,256]{1,0:T(8,128)(2,1)}, u32[]{:S(2)}) copy-start(bf16[64,256]{1,0:T(8,128)(2,1)} %get-tuple-element.5) | copy-start | bytes 98308

commit v2 on v0

v2 whole, which is shorter than its diff:
```python
import functools

import jax
import jax.numpy as jnp
from jax import lax
from jax.experimental import pallas as pl
from jax.experimental.pallas import tpu as pltpu
from jax.sharding import PartitionSpec as P

MESH = pl.DeviceIdType.MESH
F32 = jnp.float32
BF16 = jnp.bfloat16
HEAD = 128
HEADS = 8
NY, NZ, NX, NK = 4, 8, 4, 2
BLK = 768
ROWS = 16
WIDE = HEADS * HEAD
MSG = WIDE + 128
HELD = BLK + ROWS
KEYS = BLK + 128
PIECE = 2 * BLK // NZ
UNIT = 384
UNITS = HEADS * (BLK // UNIT)
HALF = NZ * ROWS // 2
FEATS = 256
C2 = HEAD**-0.5 * 1.4426950408889634
NEG = -1e30
FAR_FIRST = (4, 3, 5, 2, 6, 1, 7)


def dot(a, b):
    return jnp.dot(a, b, preferred_element_type=F32)


def kernel(
    cq, ck, cv, pq, pk, pv, w,
    enc, ans,
    q_v, kall, vall, wall, kt, kta, vaa, om, out_v,
    qz, qst, po, pm, att, anc, r3s, r3d,
    pacc, pgot, fsend, fgot,
    loc, q_ss, q_rr, k_ss, k_rr, v_ss, v_rr, w_ss, w_rr,
    n_ss, n_ys, n_zs, n_rr, r3_ss, r3_rr, a_ss, a_rr, c_ss, c_rr, f_ss, f_rr,
):
    c = lax.axis_index("ctx")
    t = lax.axis_index("tp")
    y, z = c // NZ, c % NZ
    x, core = t // NK, t % NK
    up, down, far = (y + 1) % NY, (y + NY - 1) % NY, (y + 2) % NY

    def remote(src, dst, ss, rr, dev):
        return pltpu.make_async_remote_copy(
            src_ref=src, dst_ref=dst, send_sem=ss, recv_sem=rr,
            device_id=dev, device_id_type=MESH,
        )

    def arrived(ref, sem):
        pltpu.make_async_copy(ref, ref, sem).wait()

    def at_z(d):
        return (y * NZ + (z + d) % NZ, t)

    def at_y(row):
        return (row * NZ + z, t)

    local_q = pltpu.make_async_copy(pq, qz.at[z], loc.at[0])
    local_kv = [
        pltpu.make_async_copy(ck, kall.at[y, pl.ds(0, BLK)], loc.at[1]),
        pltpu.make_async_copy(pk, kall.at[y, pl.ds(BLK, ROWS)], loc.at[2]),
        pltpu.make_async_copy(cv, vall.at[y, pl.ds(0, BLK), pl.ds(0, HEAD)], loc.at[3]),
        pltpu.make_async_copy(pv, vall.at[y, pl.ds(BLK, ROWS), pl.ds(0, HEAD)], loc.at[4]),
    ]
    local_rest = [
        pltpu.make_async_copy(cq, q_v, loc.at[5]),
        pltpu.make_async_copy(w, wall.at[y], loc.at[6]),
    ]
    local_q.start()
    for copy in local_kv + local_rest:
        copy.start()

    barrier = pltpu.get_barrier_semaphore()

    def greet(dev):
        pl.semaphore_signal(barrier, inc=1, device_id=dev, device_id_type=MESH)

    for d in range(1, NZ):
        greet(at_z(d))
    greet(at_y(up))
    greet(at_y(down))
    greet((c, x * NK + 1 - core))
    for other in range(NX):
        @pl.when((other != x) | (x != y))
        def _(other=other):
            greet((x * NZ + z, other * NK + core))
    pl.semaphore_wait(barrier, NZ - 1 + 2 + 1 + NY - jnp.where(x == y, 1, 0))

    def q_send(d):
        return remote(qz.at[z], qz.at[z], q_ss.at[d], q_rr.at[z], at_z(d))

    local_q.wait()
    for d in FAR_FIRST:
        q_send(d).start()

    def root_send(p):
        if p < NZ // 2:
            src = ck.at[pl.ds(p * PIECE, PIECE)]
        else:
            src = cv.at[pl.ds((p - NZ // 2) * PIECE, PIECE)]
        return remote(src, anc.at[p], n_ss.at[p], n_rr.at[p], (p, t))

    def anchor_y(row, i):
        return remote(anc.at[z], anc.at[z], n_ys.at[i], n_rr.at[z], at_y(row))

    def anchor_z(d):
        return remote(anc.at[z], anc.at[z], n_zs.at[d], n_rr.at[z], at_z(d))

    root_own = pltpu.make_async_copy(ck.at[pl.ds(0, PIECE)], anc.at[0], loc.at[7])

    @pl.when(c == 0)
    def _():
        root_own.start()
        for p in FAR_FIRST:
            root_send(p).start()

    def anchor_step():
        @pl.when(c == 0)
        def _():
            root_own.wait()

        @pl.when(c != 0)
        def _():
            arrived(anc.at[z], n_rr.at[z])

        @pl.when(y == 0)
        def _():
            anchor_y(1, 0).start()
            anchor_y(3, 1).start()

        @pl.when(y == 1)
        def _():
            anchor_y(2, 0).start()

        for d in FAR_FIRST:
            anchor_z(d).start()

    def keys_of(row):
        return kall.at[row, pl.ds(0, HELD)]

    def values_of(row):
        return vall.at[row, pl.ds(0, HELD), pl.ds(0, HEAD)]

    def k_send(row, to, i):
        return remote(keys_of(row), keys_of(row), k_ss.at[i], k_rr.at[row], at_y(to))

    def v_send(row, to, i):
        return remote(values_of(row), values_of(row), v_ss.at[i], v_rr.at[row], at_y(to))

    for copy in local_kv:
        copy.wait()
    k_send(y, up, 0).start()
    v_send(y, down, 1).start()
    v_send(y, up, 0).start()
    k_send(y, down, 1).start()

    W_ROWS = WIDE // 2

    def w_send(part, row, to, i):
        ref = wall.at[row, pl.ds(part * W_ROWS, W_ROWS)]
        return remote(ref, ref, w_ss.at[part, i], w_rr.at[part, row], at_y(to))

    def w_wait(part, row):
        arrived(wall.at[row, pl.ds(part * W_ROWS, W_ROWS)], w_rr.at[part, row])

    for b in range(NY):
        kall[b, HELD:] = jnp.zeros((KEYS - HELD, HEAD), BF16)
        vall[b, HELD:, :HEAD] = jnp.zeros((KEYS - HELD, HEAD), BF16)
        vall[b, :, HEAD:] = jnp.ones((KEYS, HEAD), BF16)
    vaa[:, HEAD:] = jnp.ones((BLK, HEAD), BF16)
    po[...] = jnp.zeros(po.shape, F32)
    pm[...] = jnp.full(pm.shape, NEG, F32)
    kt[y] = kall[y].T
    for copy in local_rest:
        copy.wait()

    def own_head(h):
        cols = pl.ds(pl.multiple_of(h * HEAD, HEAD), HEAD)
        r = 256
        row = lax.broadcasted_iota(jnp.int32, (r, r), 0)
        col = lax.broadcasted_iota(jnp.int32, (r, r), 1)
        tiles = range(BLK // r)
        scores = []
        for i in tiles:
            s = dot(q_v[r * i : r * (i + 1), cols], kt[y, :, : r * (i + 1)])
            last = jnp.where(col <= row, s[:, r * i :], NEG)
            scores.append(jnp.concatenate([s[:, : r * i], last], axis=1) if i else last)
        maxima = [jnp.max(s, axis=1, keepdims=True) for s in scores]
        weights = [jnp.exp2(s * C2 - m * C2).astype(BF16) for s, m in zip(scores, maxima)]
        for i in tiles:
            om[h, r * i : r * (i + 1), : 2 * HEAD] = dot(weights[i], vall[y, : r * (i + 1)])
            om[h, r * i : r * (i + 1), 2 * HEAD :] = jnp.broadcast_to(maxima[i], (r, HEAD))

    def loop_a(j, carry):
        own_head(j)

        @pl.when(j == 3)
        def _():
            arrived(keys_of(down), k_rr.at[down])
            k_send(down, up, 2).start()
            arrived(values_of(up), v_rr.at[up])
            v_send(up, down, 2).start()

        @pl.when(((j == 4) & (y == 0)) | ((j == 6) & (y % 2 == 1)))
        def _():
            anchor_step()

        return carry

    lax.fori_loop(0, HEADS, loop_a, 0)

    for part in range(2):
        w_send(part, y, up, 0).start()
        w_send(part, y, down, 1).start()

    def turn(j):
        return (z + 2 + j) % NZ

    for d in range(1, NZ):
        arrived(qz.at[(z + d) % NZ], q_rr.at[(z + d) % NZ])
    for j in range(NZ):
        for h in range(HEADS):
            qst[(j * HEADS + h) * ROWS : (j * HEADS + h + 1) * ROWS] = qz[turn(j), :, HEAD * h : HEAD * (h + 1)]
    arrived(values_of(down), v_rr.at[down])
    arrived(keys_of(up), k_rr.at[up])
    kt[down] = kall[down].T
    kt[up] = kall[up].T

    QUAD = 4
    STACK = HEADS * ROWS

    def prompt(s_at, carry):
        a, i = s_at // NY, s_at % NY
        b = (y + jnp.where(i == 0, 0, jnp.where(i == 1, 3, i - 1))) % NY

        @pl.when((s_at == 2) & (y == 2))
        def _():
            anchor_step()

        @pl.when(s_at == 3)
        def _():
            arrived(keys_of(far), k_rr.at[far])
            arrived(values_of(far), v_rr.at[far])
            kt[far] = kall[far].T

        rows = pl.ds(pl.multiple_of(a * (QUAD * STACK), QUAD * STACK), QUAD * STACK)
        s = dot(qst[rows], kt[b])
        r = lax.broadcasted_iota(jnp.int32, (STACK, 128), 0) % ROWS
        k = lax.broadcasted_iota(jnp.int32, (STACK, 128), 1)
        last = []
        for g in range(QUAD):
            ahead = (y * NZ + turn(a * QUAD + g) - (b * NZ + z)) * ROWS
            last.append(jnp.where((k < ROWS) & (k <= r + ahead), s[STACK * g : STACK * (g + 1), BLK:], NEG))
        s = jnp.concatenate([s[:, :BLK], jnp.concatenate(last, axis=0)], axis=1)
        m = jnp.max(s, axis=1, keepdims=True) * C2
        o = dot(jnp.exp2(s * C2 - m).astype(BF16), vall[b])
        old = pm[rows]
        top = jnp.maximum(old, m)
        f_old, f = jnp.exp2(old - top), jnp.exp2(m - top)
        pm[rows] = top
        po[rows, :HEAD] = po[rows, :HEAD] * f_old + o[:, :HEAD] * f
        po[rows, HEAD:] = po[rows, HEAD:] * f_old + o[:, HEAD:] * f

        @pl.when(i == NY - 1)
        def _():
            for g in range(QUAD):
                send_partial(a * QUAD + g)

        return carry

    lane = lax.broadcasted_iota(jnp.int32, (ROWS, 128), 1)

    def r3_send(j):
        return remote(r3s.at[j], r3d.at[j], r3_ss.at[j], r3_rr.at[j], at_z(2 + j))

    def send_partial(j):
        stats = jnp.zeros((ROWS, 128), F32)
        for h in range(HEADS):
            rows = pl.ds(pl.multiple_of((j * HEADS + h) * ROWS, ROWS), ROWS)
            m = pm[rows]
            even = jnp.ceil(m * 0.25) * 4
            f = jnp.exp2(m - even)
            r3s[j, :, HEAD * h : HEAD * (h + 1)] = (po[rows, :HEAD] * f).astype(BF16)
            total = po[rows, HEAD:] * f
            high = total.astype(BF16).astype(F32)
            stats = jnp.where(lane == h, high, stats)
            stats = jnp.where(lane == 8 + h, total - high, stats)
            stats = jnp.where(lane == 16 + h, even, stats)
        r3s[j, :, WIDE:] = stats.astype(BF16)

        @pl.when(j != 6)
        def _():
            r3_send(j).start()

    lax.fori_loop(0, 2 * NY, prompt, 0)

    w_wait(0, down)
    w_send(0, down, up, 2).start()
    w_wait(1, up)
    w_send(1, up, down, 2).start()

    for d in range(1, NZ):
        arrived(anc.at[(z + d) % NZ], n_rr.at[(z + d) % NZ])
    for p in range(NZ // 2):
        kta[:, PIECE * p : PIECE * (p + 1)] = anc[p].T
        vaa[PIECE * p : PIECE * (p + 1), :HEAD] = anc[NZ // 2 + p]

    seen = jnp.where(c > 0, 0.0, NEG)

    def anchor_unit(u, carry):
        h, i = u // (BLK // UNIT), u % (BLK // UNIT)
        cols = pl.ds(pl.multiple_of(h * HEAD, HEAD), HEAD)
        rows = pl.ds(pl.multiple_of(i * UNIT, UNIT), UNIT)
        s = dot(q_v[rows, cols], kta[...])
        m = jnp.max(s, axis=1, keepdims=True)
        o = dot(jnp.exp2(s * C2 - m * C2).astype(BF16), vaa[...])
        m = m + seen
        own = om[h, rows, 2 * HEAD :]
        top = jnp.maximum(m, own)
        f_own, f = jnp.exp2((own - top) * C2), jnp.exp2((m - top) * C2)
        above = om[h, rows, :HEAD] * f_own + o[:, :HEAD] * f
        below = om[h, rows, HEAD : 2 * HEAD] * f_own + o[:, HEAD:] * f
        out_v[rows, cols] = (above / below).astype(BF16)
        return carry

    lax.fori_loop(0, RS_UNITS, anchor_unit, 0)

    for j in range(NZ):
        if j != 6:
            arrived(r3d.at[j], r3_rr.at[j])
    parts = [r3s if j == 6 else r3d for j in range(NZ)]
    stats = [parts[j][j, :, WIDE:].astype(F32) for j in range(NZ)]
    top = functools.reduce(jnp.maximum, stats)
    factors = [jnp.exp2(s - top) for s in stats]
    total = sum(
        (s + pltpu.roll(s, 120, 1)) * pltpu.roll(f, 112, 1) for s, f in zip(stats, factors)
    )
    for h in range(HEADS):
        cols = slice(HEAD * h, HEAD * (h + 1))
        merged = sum(
            parts[j][j, :, cols].astype(F32) * factors[j][:, 16 + h : 17 + h] for j in range(NZ)
        )
        att[z, :, cols] = (merged / total[:, h : h + 1]).astype(BF16)

    def a_send(d):
        return remote(att.at[z], att.at[z], a_ss.at[d], a_rr.at[z], at_z(d))

    for d in FAR_FIRST:
        a_send(d).start()

    lax.fori_loop(RS_UNITS, RS_UNITS + AG_UNITS, anchor_unit, 0)

    for part in range(2):
        if part == 0:
            w_wait(0, up)
            w_wait(1, down)
        w_wait(part, far)
    for d in range(1, NZ):
        arrived(att.at[(z + d) % NZ], a_rr.at[(z + d) % NZ])
    rows = jnp.concatenate([att[i] for i in range(NZ)], axis=0)
    for b in range(NY):
        part = dot(rows, wall[b])
        for i in range(2):
            pacc[i, :, FEATS * b : FEATS * (b + 1)] = part[HALF * i : HALF * (i + 1)]

    c_send = remote(pacc.at[1 - core], pgot, c_ss, c_rr, (c, x * NK + 1 - core))
    c_send.start()
    c_send.wait_recv()

    def f_send(row):
        return remote(fsend.at[row], fgot.at[x], f_ss.at[row], f_rr.at[x], (row * NZ + z, y * NK + core))

    for row in range(NY):
        cols = slice(FEATS * row, FEATS * (row + 1))
        piece = pacc[core, :, cols] + pgot[:, cols]
        home = (x == y) & (y == row)

        @pl.when(home)
        def _(piece=piece):
            fgot[x] = piece.astype(BF16)

        @pl.when(jnp.logical_not(home))
        def _(piece=piece, row=row):
            fsend[row] = piece.astype(BF16)
            f_send(row).start()

    lax.fori_loop(RS_UNITS + AG_UNITS, UNITS, anchor_unit, 0)
    enc_out = pltpu.make_async_copy(out_v, enc, loc.at[8])
    enc_out.start()

    for other in range(NX):
        @pl.when((other != x) | (x != y))
        def _(other=other):
            arrived(fgot.at[other], f_rr.at[other])
    ans[...] = sum(fgot[i].astype(F32) for i in range(NX)).astype(BF16)

    for d in range(1, NZ):
        q_send(d).wait_send()
        anchor_z(d).wait_send()
        a_send(d).wait_send()

    @pl.when(c == 0)
    def _():
        for p in range(1, NZ):
            root_send(p).wait_send()

    @pl.when(y == 0)
    def _():
        anchor_y(1, 0).wait_send()
        anchor_y(3, 1).wait_send()

    @pl.when(y == 1)
    def _():
        anchor_y(2, 0).wait_send()

    for i, row in enumerate((y, y, down)):
        k_send(row, up, i).wait_send()
        w_send(0, row, up, i).wait_send()
        w_send(1, row, up, i).wait_send()
        v_send(row, up, i).wait_send()
    for j in range(NZ):
        if j != 6:
            r3_send(j).wait_send()
    c_send.wait_send()
    for row in range(NY):
        @pl.when((x != y) | (y != row))
        def _(row=row):
            f_send(row).wait_send()
    enc_out.wait()


RS_UNITS = 6
AG_UNITS = 6


def on_device(cq, ck, cv, pq, pk, pv, w):
    vm, dma = pltpu.VMEM, pltpu.SemaphoreType.DMA
    any_space = pl.BlockSpec(memory_space=pl.ANY)
    return pl.pallas_call(
        kernel,
        out_shape=(
            jax.ShapeDtypeStruct((BLK, WIDE), BF16),
            jax.ShapeDtypeStruct((HALF, FEATS), BF16),
        ),
        in_specs=[any_space] * 7,
        out_specs=(any_space, pl.BlockSpec(memory_space=pltpu.VMEM)),
        scratch_shapes=[
            vm((BLK, WIDE), BF16), vm((NY, KEYS, HEAD), BF16), vm((NY, KEYS, 2 * HEAD), BF16),
            vm((NY, WIDE, FEATS), BF16), vm((NY, HEAD, KEYS), BF16),
            vm((HEAD, BLK), BF16), vm((BLK, 2 * HEAD), BF16),
            vm((HEADS, BLK, 3 * HEAD), F32), vm((BLK, WIDE), BF16),
            vm((NZ, ROWS, WIDE), BF16), vm((NZ * HEADS * ROWS, HEAD), BF16),
            vm((NZ * HEADS * ROWS, 2 * HEAD), F32), vm((NZ * HEADS * ROWS, HEAD), F32),
            vm((NZ, ROWS, WIDE), BF16), vm((NZ, PIECE, HEAD), BF16),
            vm((NZ, ROWS, MSG), BF16), vm((NZ, ROWS, MSG), BF16),
            vm((2, HALF, NY * FEATS), F32), vm((HALF, NY * FEATS), F32),
            vm((NY, HALF, FEATS), BF16), vm((NX, HALF, FEATS), BF16),
            dma((9,)), dma((NZ,)), dma((NZ,)), dma((3,)), dma((NY,)), dma((3,)), dma((NY,)),
            dma((2, 3)), dma((2, NY)),
            dma((NZ,)), dma((2,)), dma((NZ,)), dma((NZ,)), dma((NZ,)), dma((NZ,)),
            dma((NZ,)), dma((NZ,)), dma, dma, dma((NY,)), dma((NX,)),
        ],
        compiler_params=pltpu.CompilerParams(
            collective_id=0, has_side_effects=True, vmem_limit_bytes=56 * 2**20
        ),
        cost_estimate=pl.CostEstimate(flops=12 * 10**9, bytes_accessed=5 * 10**6, transcendentals=11 * 10**6),
        name="star",
    )(cq, ck, cv, pq, pk, pv, w)


def solution(mesh):
    placed = (P("ctx", "tp"),) * 6 + (P("tp", "ctx"),)
    return jax.shard_map(
        on_device,
        mesh=mesh,
        in_specs=placed,
        out_specs=(P("ctx", "tp"), P("tp", "ctx")),
        check_vma=False,
    )
```

time: 475 us -> 63.4 us (0.13); the launches traced: 469 us -> 63 us
  blocking collectives: 187 us -> 0 us
  waiting for transfers between devices: 173 us -> 0 us
  Pallas kernels: 0 us -> 59.1 us
  matrix products: 49.8 us -> 0 us
  other arithmetic: 19.1 us -> 0 us
  between operations: 13.9 us -> 0.65 us
  local copies, waits for them, and re-layouts: 14.4 us -> 3.29 us
  loops' own time: 11.1 us -> 0 us
    psum x2 -> x0, waiting for transfers between devices: 98.9 us -> none  [the longest x1 83.2 us: on_device(): lax.psum((accumulated * factor[..., None], row_sum * factor), 'ctx')]
    psum x1 -> x0, blocking collectives: 93.9 us -> none  [on_device(): lax.psum((accumulated * factor[..., None], row_sum * factor), 'ctx')]
    pmax x1 -> x0, blocking collectives: 93.2 us -> none  [on_device(): overall = lax.pmax(row_max, 'ctx')]
    all_gather x1 -> x0, waiting for transfers between devices: 73.6 us -> none  [on_device(): gathered = lax.all_gather(prompt_queries, 'ctx', axis=0, tiled=True)]
    pallas_call x0 -> x1, Pallas kernels: none -> 59.1 us  [on_device(): pl.pallas_call(kernel, out_shape=(jax.ShapeDtypeStruct((BLK, WIDE), BF16)...]
    dot_general x33 -> x0, matrix products: 49.8 us -> none  [the longest x16 26.8 us: head_partial(): jnp.dot(query_rows, key_rows.T, preferred_element_type=jnp.float32)]
    another operation x2 -> x0, loops' own time: 11.1 us -> none  [the longest x1 5.77 us: on_device(): lax.map(prompt_head, jnp.arange(head_count, dtype=jnp.int32))]
    dynamic_slice x16 -> x0, local copies, waits for them, and re-layouts: 9.94 us -> none  [on_device(): per_head = lax.map(encode_head, jnp.arange(head_count, dtype=jnp.int32))]
  transfers between devices with their start and end apart: 4 -> 0, of which waited for: 3 -> 0; matrix products, arithmetic and copies ran while one was open for 17% -> 0% of each run, Pallas kernels for 0% -> 0%
where the time goes in v2:
time: 63.4 us; the launch traced here: 63 us
  Pallas kernels  59.1 us (93%)
  local copies, waits for them, and re-layouts  3.29 us (5%)
  between operations  0.65 us (1%)
    pallas_call x1, Pallas kernels, on_device(): pl.pallas_call(kernel, out_shape=(jax.ShapeDtypeStruct((BLK, WIDE), BF16)...  59.1 us
    unnamed x4, local copies, waits for them, and re-layouts  3.29 us

profile of v2, /device:TPU:17, one launch (start us, length us, event | category | flops | bytes accessed | tf_op | source)
XLA Modules:
  0.0 63.0 jit_solution(17951716889592648089)
XLA Ops:
  0.6 59.1 %star.1 = (bf16[768,1024]{1,0:T(8,128)(2,1)}, bf16[64,256]{1,0:T(8,128)(2,1)}) custom-call(bf16[768,1024]{1,0:T(8,128)(2,1)} %cq.1, bf16[768,128]{1,0:T(8,128)(2,1)} %ck.1, bf16[768,128]{1,0:T(8,128)(2,1)} %cv.1, bf16[16,1024]{1,0:T(8,128)(2,1)} %pq.1, bf16[16,128]{1,0:T(8,128)(2,1)} %pk.1, bf16[16,128]{1,0:T(8,128)(2,1)} %pv.1, bf16[1024,256]{1,0:T(8,128)(2,1)} %w.1), custom_call_target="tpu_custom_call" | custom-call | flops 12000000000 | bytes 5000000 | tf_op jit(solution)/shard_map/star/pallas_call | solution.py:447
  59.7 0.0 copy-start
  59.7 2.7 %copy.11 = bf16[768,1024]{1,0:T(8,128)(2,1)} copy(bf16[768,1024]{1,0:T(8,128)(2,1)} %get-tuple-element.4) | data formatting | bytes 3145728
  62.4 0.0 copy-done
  62.4 0.6 copy.12
Async XLA Ops:
  59.7 2.7 %copy-start = (bf16[64,256]{1,0:T(8,128)(2,1)S(1)}, bf16[64,256]{1,0:T(8,128)(2,1)}, u32[]{:S(2)}) copy-start(bf16[64,256]{1,0:T(8,128)(2,1)} %get-tuple-element.5) | copy-start | bytes 98308

commit v3 on v2

--- a/solution.py
+++ b/solution.py
@@ -20,8 +20,9 @@
 HELD = BLK + ROWS
 KEYS = BLK + 128
 PIECE = 2 * BLK // NZ
-UNIT = 384
-UNITS = HEADS * (BLK // UNIT)
+QUARTER = PIECE // NY
+EARLY = 3
+AG_UNITS = 3
 HALF = NZ * ROWS // 2
 FEATS = 256
 C2 = HEAD**-0.5 * 1.4426950408889634
@@ -36,11 +37,11 @@
 def kernel(
     cq, ck, cv, pq, pk, pv, w,
     enc, ans,
-    q_v, kall, vall, wall, kt, kta, vaa, om, out_v,
-    qz, qst, po, pm, att, anc, r3s, r3d,
+    q_v, kall, vgot, vall, wall, kt, kta, vaa, om, out_v,
+    qz, qst, po, pm, att, stage, anc, r3s, r3d,
     pacc, pgot, fsend, fgot,
     loc, q_ss, q_rr, k_ss, k_rr, v_ss, v_rr, w_ss, w_rr,
-    n_ss, n_ys, n_zs, n_rr, r3_ss, r3_rr, a_ss, a_rr, c_ss, c_rr, f_ss, f_rr,
+    n_ss, n_qs, n_zs, n_ys, n_rr, n_zr, n_yr, r3_ss, r3_rr, a_ss, a_rr, c_ss, c_rr, f_ss, f_rr,
 ):
     c = lax.axis_index("ctx")
     t = lax.axis_index("tp")
@@ -67,8 +68,8 @@
     local_kv = [
         pltpu.make_async_copy(ck, kall.at[y, pl.ds(0, BLK)], loc.at[1]),
         pltpu.make_async_copy(pk, kall.at[y, pl.ds(BLK, ROWS)], loc.at[2]),
-        pltpu.make_async_copy(cv, vall.at[y, pl.ds(0, BLK), pl.ds(0, HEAD)], loc.at[3]),
-        pltpu.make_async_copy(pv, vall.at[y, pl.ds(BLK, ROWS), pl.ds(0, HEAD)], loc.at[4]),
+        pltpu.make_async_copy(cv, vgot.at[y, pl.ds(0, BLK)], loc.at[3]),
+        pltpu.make_async_copy(pv, vgot.at[y, pl.ds(BLK, ROWS)], loc.at[4]),
     ]
     local_rest = [
         pltpu.make_async_copy(cq, q_v, loc.at[5]),
@@ -87,34 +88,35 @@
         greet(at_z(d))
     greet(at_y(up))
     greet(at_y(down))
+    greet(at_y(far))
     greet((c, x * NK + 1 - core))
     for other in range(NX):
         @pl.when((other != x) | (x != y))
         def _(other=other):
             greet((x * NZ + z, other * NK + core))
-    pl.semaphore_wait(barrier, NZ - 1 + 2 + 1 + NY - jnp.where(x == y, 1, 0))
+    pl.semaphore_wait(barrier, NZ - 1 + 3 + 1 + NY - jnp.where(x == y, 1, 0))
 
     def q_send(d):
         return remote(qz.at[z], qz.at[z], q_ss.at[d], q_rr.at[z], at_z(d))
 
-    local_q.wait()
-    for d in FAR_FIRST:
-        q_send(d).start()
 
     def root_send(p):
         if p < NZ // 2:
             src = ck.at[pl.ds(p * PIECE, PIECE)]
         else:
             src = cv.at[pl.ds((p - NZ // 2) * PIECE, PIECE)]
-        return remote(src, anc.at[p], n_ss.at[p], n_rr.at[p], (p, t))
+        return remote(src, stage, n_ss.at[p], n_rr.at[0], (p, t))
+
+    def quarter_send(row):
+        return remote(stage.at[pl.ds(row * QUARTER, QUARTER)], anc.at[row, z], n_qs.at[row], n_rr.at[1], at_y(row))
+
+    def anchor_z(d):
+        return remote(anc.at[y, z], anc.at[y, z], n_zs.at[d], n_zr.at[z], at_z(d))
 
     def anchor_y(row, i):
-        return remote(anc.at[z], anc.at[z], n_ys.at[i], n_rr.at[z], at_y(row))
-
-    def anchor_z(d):
-        return remote(anc.at[z], anc.at[z], n_zs.at[d], n_rr.at[z], at_z(d))
-
-    root_own = pltpu.make_async_copy(ck.at[pl.ds(0, PIECE)], anc.at[0], loc.at[7])
+        return remote(anc.at[y], anc.at[y], n_ys.at[i], n_yr.at[y], at_y(row))
+
+    root_own = pltpu.make_async_copy(ck.at[pl.ds(0, PIECE)], stage, loc.at[7])
 
     @pl.when(c == 0)
     def _():
@@ -122,32 +124,44 @@
         for p in FAR_FIRST:
             root_send(p).start()
 
-    def anchor_step():
+    local_q.wait()
+    for d in FAR_FIRST:
+        q_send(d).start()
+
+    def anchor_quarters():
         @pl.when(c == 0)
         def _():
             root_own.wait()
 
         @pl.when(c != 0)
         def _():
-            arrived(anc.at[z], n_rr.at[z])
-
-        @pl.when(y == 0)
-        def _():
-            anchor_y(1, 0).start()
-            anchor_y(3, 1).start()
-
-        @pl.when(y == 1)
-        def _():
-            anchor_y(2, 0).start()
-
+            arrived(stage, n_rr.at[0])
+
+        for row in (2, 1, 3):
+            quarter_send(row).start()
+        anc[0, z] = stage[:QUARTER]
         for d in FAR_FIRST:
             anchor_z(d).start()
 
+    def anchor_along_z():
+        arrived(anc.at[y, z], n_rr.at[1])
+        for d in FAR_FIRST:
+            anchor_z(d).start()
+
+    def anchor_along_y():
+        for d in range(1, NZ):
+            arrived(anc.at[y, (z + d) % NZ], n_zr.at[(z + d) % NZ])
+        for i, row in enumerate((far, up, down)):
+            anchor_y(row, i).start()
+
     def keys_of(row):
         return kall.at[row, pl.ds(0, HELD)]
 
     def values_of(row):
-        return vall.at[row, pl.ds(0, HELD), pl.ds(0, HEAD)]
+        return vgot.at[row]
+
+    def spread_values(row):
+        vall[row, :HELD, :HEAD] = vgot[row]
 
     def k_send(row, to, i):
         return remote(keys_of(row), keys_of(row), k_ss.at[i], k_rr.at[row], at_y(to))
@@ -179,6 +193,7 @@
     po[...] = jnp.zeros(po.shape, F32)
     pm[...] = jnp.full(pm.shape, NEG, F32)
     kt[y] = kall[y].T
+    spread_values(y)
     for copy in local_rest:
         copy.wait()
 
@@ -200,26 +215,25 @@
             om[h, r * i : r * (i + 1), 2 * HEAD :] = jnp.broadcast_to(maxima[i], (r, HEAD))
 
     def loop_a(j, carry):
-        own_head(j)
-
-        @pl.when(j == 3)
-        def _():
-            arrived(keys_of(down), k_rr.at[down])
-            k_send(down, up, 2).start()
-            arrived(values_of(up), v_rr.at[up])
-            v_send(up, down, 2).start()
-
-        @pl.when(((j == 4) & (y == 0)) | ((j == 6) & (y % 2 == 1)))
-        def _():
-            anchor_step()
+        own_head(2 * j)
+        own_head(2 * j + 1)
 
         return carry
 
-    lax.fori_loop(0, HEADS, loop_a, 0)
-
-    for part in range(2):
-        w_send(part, y, up, 0).start()
-        w_send(part, y, down, 1).start()
+    lax.fori_loop(0, EARLY, loop_a, 0)
+    arrived(keys_of(down), k_rr.at[down])
+    k_send(down, up, 2).start()
+    arrived(values_of(up), v_rr.at[up])
+    v_send(up, down, 2).start()
+
+    @pl.when(y == 0)
+    def _():
+        anchor_quarters()
+
+    w_send(0, y, up, 0).start()
+    w_send(1, y, down, 1).start()
+    w_send(1, y, up, 0).start()
+    w_send(0, y, down, 1).start()
 
     def turn(j):
         return (z + 2 + j) % NZ
@@ -229,50 +243,64 @@
     for j in range(NZ):
         for h in range(HEADS):
             qst[(j * HEADS + h) * ROWS : (j * HEADS + h + 1) * ROWS] = qz[turn(j), :, HEAD * h : HEAD * (h + 1)]
-    arrived(values_of(down), v_rr.at[down])
-    arrived(keys_of(up), k_rr.at[up])
     kt[down] = kall[down].T
-    kt[up] = kall[up].T
 
     QUAD = 4
     STACK = HEADS * ROWS
 
-    def prompt(s_at, carry):
-        a, i = s_at // NY, s_at % NY
-        b = (y + jnp.where(i == 0, 0, jnp.where(i == 1, 3, i - 1))) % NY
-
-        @pl.when((s_at == 2) & (y == 2))
-        def _():
-            anchor_step()
-
-        @pl.when(s_at == 3)
+    def prompt(i, carry):
+        halves = (i // 3, jnp.where((i == 0) | (i > 1), 1, 0))
+        steps = (jnp.where(i == 0, 0, jnp.where(i == 1, 3, jnp.where(i == 2, 2, 1))),
+                 jnp.where(i == 0, 0, jnp.where(i == 1, 1, jnp.where(i == 2, 3, 2))))
+
+        @pl.when(i == 1)
+        def _():
+            arrived(values_of(down), v_rr.at[down])
+            arrived(keys_of(up), k_rr.at[up])
+            kt[up] = kall[up].T
+            spread_values(down)
+            spread_values(up)
+
+        @pl.when(i == 2)
         def _():
             arrived(keys_of(far), k_rr.at[far])
             arrived(values_of(far), v_rr.at[far])
             kt[far] = kall[far].T
-
-        rows = pl.ds(pl.multiple_of(a * (QUAD * STACK), QUAD * STACK), QUAD * STACK)
-        s = dot(qst[rows], kt[b])
+            spread_values(far)
+
+        @pl.when((i == 2) & (y != 0))
+        def _():
+            anchor_along_z()
+
         r = lax.broadcasted_iota(jnp.int32, (STACK, 128), 0) % ROWS
         k = lax.broadcasted_iota(jnp.int32, (STACK, 128), 1)
-        last = []
-        for g in range(QUAD):
-            ahead = (y * NZ + turn(a * QUAD + g) - (b * NZ + z)) * ROWS
-            last.append(jnp.where((k < ROWS) & (k <= r + ahead), s[STACK * g : STACK * (g + 1), BLK:], NEG))
-        s = jnp.concatenate([s[:, :BLK], jnp.concatenate(last, axis=0)], axis=1)
-        m = jnp.max(s, axis=1, keepdims=True) * C2
-        o = dot(jnp.exp2(s * C2 - m).astype(BF16), vall[b])
-        old = pm[rows]
-        top = jnp.maximum(old, m)
-        f_old, f = jnp.exp2(old - top), jnp.exp2(m - top)
-        pm[rows] = top
-        po[rows, :HEAD] = po[rows, :HEAD] * f_old + o[:, :HEAD] * f
-        po[rows, HEAD:] = po[rows, HEAD:] * f_old + o[:, HEAD:] * f
-
-        @pl.when(i == NY - 1)
-        def _():
+        pairs = [
+            (a, (y + step) % NY, pl.ds(pl.multiple_of(a * (QUAD * STACK), QUAD * STACK), QUAD * STACK))
+            for a, step in zip(halves, steps)
+        ]
+        scores = []
+        for a, b, rows in pairs:
+            s = dot(qst[rows], kt[b])
+            last = []
             for g in range(QUAD):
-                send_partial(a * QUAD + g)
+                ahead = (y * NZ + turn(a * QUAD + g) - (b * NZ + z)) * ROWS
+                last.append(jnp.where((k < ROWS) & (k <= r + ahead), s[STACK * g : STACK * (g + 1), BLK:], NEG))
+            scores.append(jnp.concatenate([s[:, :BLK], jnp.concatenate(last, axis=0)], axis=1))
+        maxima = [jnp.max(s, axis=1, keepdims=True) * C2 for s in scores]
+        weights = [jnp.exp2(s * C2 - m).astype(BF16) for s, m in zip(scores, maxima)]
+        results = [dot(p, vall[b]) for p, (_, b, _) in zip(weights, pairs)]
+        for (_, _, rows), m, o in zip(pairs, maxima, results):
+            old = pm[rows]
+            top = jnp.maximum(old, m)
+            f_old, f = jnp.exp2(old - top), jnp.exp2(m - top)
+            pm[rows] = top
+            po[rows, :HEAD] = po[rows, :HEAD] * f_old + o[:, :HEAD] * f
+            po[rows, HEAD:] = po[rows, HEAD:] * f_old + o[:, HEAD:] * f
+
+        @pl.when(i >= 2)
+        def _():
+            for g in range(QUAD):
+                send_partial((i - 2) * QUAD + g)
 
         return carry
 
@@ -300,38 +328,25 @@
         def _():
             r3_send(j).start()
 
-    lax.fori_loop(0, 2 * NY, prompt, 0)
-
-    w_wait(0, down)
-    w_send(0, down, up, 2).start()
-    w_wait(1, up)
-    w_send(1, up, down, 2).start()
-
-    for d in range(1, NZ):
-        arrived(anc.at[(z + d) % NZ], n_rr.at[(z + d) % NZ])
-    for p in range(NZ // 2):
-        kta[:, PIECE * p : PIECE * (p + 1)] = anc[p].T
-        vaa[PIECE * p : PIECE * (p + 1), :HEAD] = anc[NZ // 2 + p]
+    lax.fori_loop(0, 4, prompt, 0)
+    anchor_along_y()
+    lax.fori_loop(EARLY, HEADS // 2, loop_a, 0)
 
     seen = jnp.where(c > 0, 0.0, NEG)
 
-    def anchor_unit(u, carry):
-        h, i = u // (BLK // UNIT), u % (BLK // UNIT)
+    def anchor_unit(h, carry):
         cols = pl.ds(pl.multiple_of(h * HEAD, HEAD), HEAD)
-        rows = pl.ds(pl.multiple_of(i * UNIT, UNIT), UNIT)
-        s = dot(q_v[rows, cols], kta[...])
+        s = dot(q_v[:, cols], kta[...])
         m = jnp.max(s, axis=1, keepdims=True)
         o = dot(jnp.exp2(s * C2 - m * C2).astype(BF16), vaa[...])
         m = m + seen
-        own = om[h, rows, 2 * HEAD :]
+        own = om[h, :, 2 * HEAD :]
         top = jnp.maximum(m, own)
         f_own, f = jnp.exp2((own - top) * C2), jnp.exp2((m - top) * C2)
-        above = om[h, rows, :HEAD] * f_own + o[:, :HEAD] * f
-        below = om[h, rows, HEAD : 2 * HEAD] * f_own + o[:, HEAD:] * f
-        out_v[rows, cols] = (above / below).astype(BF16)
+        above = om[h, :, :HEAD] * f_own + o[:, :HEAD] * f
+        below = om[h, :, HEAD : 2 * HEAD] * f_own + o[:, HEAD:] * f
+        out_v[:, cols] = (above / below).astype(BF16)
         return carry
-
-    lax.fori_loop(0, RS_UNITS, anchor_unit, 0)
 
     for j in range(NZ):
         if j != 6:
@@ -356,7 +371,24 @@
     for d in FAR_FIRST:
         a_send(d).start()
 
-    lax.fori_loop(RS_UNITS, RS_UNITS + AG_UNITS, anchor_unit, 0)
+    w_wait(0, down)
+    w_send(0, down, up, 2).start()
+    w_wait(1, up)
+    w_send(1, up, down, 2).start()
+
+    for row in (up, down, far):
+        arrived(anc.at[row], n_yr.at[row])
+    for i in range(NY):
+        at = slice(PIECE * i, PIECE * (i + 1))
+        kta[:, at] = jnp.concatenate([anc[i, p] for p in range(NZ // 2)], axis=0).T
+        vaa[at, :HEAD] = jnp.concatenate([anc[i, NZ // 2 + p] for p in range(NZ // 2)], axis=0)
+
+    lax.fori_loop(0, AG_UNITS, anchor_unit, 0)
+    enc_out = [
+        pltpu.make_async_copy(out_v.at[:, cols], enc.at[:, cols], loc.at[8 + i])
+        for i, cols in enumerate((pl.ds(0, AG_UNITS * HEAD), pl.ds(AG_UNITS * HEAD, (HEADS - AG_UNITS) * HEAD)))
+    ]
+    enc_out[0].start()
 
     for part in range(2):
         if part == 0:
@@ -392,9 +424,8 @@
             fsend[row] = piece.astype(BF16)
             f_send(row).start()
 
-    lax.fori_loop(RS_UNITS + AG_UNITS, UNITS, anchor_unit, 0)
-    enc_out = pltpu.make_async_copy(out_v, enc, loc.at[8])
-    enc_out.start()
+    lax.fori_loop(AG_UNITS, HEADS, anchor_unit, 0)
+    enc_out[1].start()
 
     for other in range(NX):
         @pl.when((other != x) | (x != y))
@@ -414,12 +445,11 @@
 
     @pl.when(y == 0)
     def _():
-        anchor_y(1, 0).wait_send()
-        anchor_y(3, 1).wait_send()
-
-    @pl.when(y == 1)
-    def _():
-        anchor_y(2, 0).wait_send()
+        for row in (2, 1, 3):
+            quarter_send(row).wait_send()
+
+    for i, row in enumerate((far, up, down)):
+        anchor_y(row, i).wait_send()
 
     for i, row in enumerate((y, y, down)):
         k_send(row, up, i).wait_send()
@@ -434,17 +464,34 @@
         @pl.when((x != y) | (y != row))
         def _(row=row):
             f_send(row).wait_send()
-    enc_out.wait()
-
-
-RS_UNITS = 6
-AG_UNITS = 6
+    for copy in enc_out:
+        copy.wait()
+
+
+PARTS = 4
+
+
+def publish(enc, ans, enc_out, ans_out, held, held_ans, into, out):
+    tall = BLK // PARTS
+    pairs = [(ans, held_ans, ans_out)]
+    for i in range(PARTS):
+        rows = pl.ds(tall * i, tall)
+        pairs.append((enc.at[rows], held.at[rows], enc_out.at[rows]))
+    reads = [pltpu.make_async_copy(src, mid, into.at[i]) for i, (src, mid, _) in enumerate(pairs)]
+    writes = [pltpu.make_async_copy(mid, dst, out.at[i]) for i, (_, mid, dst) in enumerate(pairs)]
+    for copy in reads:
+        copy.start()
+    for read, write in zip(reads, writes):
+        read.wait()
+        write.start()
+    for copy in writes:
+        copy.wait()
 
 
 def on_device(cq, ck, cv, pq, pk, pv, w):
     vm, dma = pltpu.VMEM, pltpu.SemaphoreType.DMA
     any_space = pl.BlockSpec(memory_space=pl.ANY)
-    return pl.pallas_call(
+    results = pl.pallas_call(
         kernel,
         out_shape=(
             jax.ShapeDtypeStruct((BLK, WIDE), BF16),
@@ -453,19 +500,19 @@
         in_specs=[any_space] * 7,
         out_specs=(any_space, pl.BlockSpec(memory_space=pltpu.VMEM)),
         scratch_shapes=[
-            vm((BLK, WIDE), BF16), vm((NY, KEYS, HEAD), BF16), vm((NY, KEYS, 2 * HEAD), BF16),
+            vm((BLK, WIDE), BF16), vm((NY, KEYS, HEAD), BF16), vm((NY, HELD, HEAD), BF16), vm((NY, KEYS, 2 * HEAD), BF16),
             vm((NY, WIDE, FEATS), BF16), vm((NY, HEAD, KEYS), BF16),
             vm((HEAD, BLK), BF16), vm((BLK, 2 * HEAD), BF16),
             vm((HEADS, BLK, 3 * HEAD), F32), vm((BLK, WIDE), BF16),
             vm((NZ, ROWS, WIDE), BF16), vm((NZ * HEADS * ROWS, HEAD), BF16),
             vm((NZ * HEADS * ROWS, 2 * HEAD), F32), vm((NZ * HEADS * ROWS, HEAD), F32),
-            vm((NZ, ROWS, WIDE), BF16), vm((NZ, PIECE, HEAD), BF16),
+            vm((NZ, ROWS, WIDE), BF16), vm((PIECE, HEAD), BF16), vm((NY, NZ, QUARTER, HEAD), BF16),
             vm((NZ, ROWS, MSG), BF16), vm((NZ, ROWS, MSG), BF16),
             vm((2, HALF, NY * FEATS), F32), vm((HALF, NY * FEATS), F32),
             vm((NY, HALF, FEATS), BF16), vm((NX, HALF, FEATS), BF16),
-            dma((9,)), dma((NZ,)), dma((NZ,)), dma((3,)), dma((NY,)), dma((3,)), dma((NY,)),
+            dma((10,)), dma((NZ,)), dma((NZ,)), dma((3,)), dma((NY,)), dma((3,)), dma((NY,)),
             dma((2, 3)), dma((2, NY)),
-            dma((NZ,)), dma((2,)), dma((NZ,)), dma((NZ,)), dma((NZ,)), dma((NZ,)),
+            dma((NZ,)), dma((NY,)), dma((NZ,)), dma((3,)), dma((2,)), dma((NZ,)), dma((NY,)), dma((NZ,)), dma((NZ,)),
             dma((NZ,)), dma((NZ,)), dma, dma, dma((NY,)), dma((NX,)),
         ],
         compiler_params=pltpu.CompilerParams(
@@ -474,6 +521,15 @@
         cost_estimate=pl.CostEstimate(flops=12 * 10**9, bytes_accessed=5 * 10**6, transcendentals=11 * 10**6),
         name="star",
     )(cq, ck, cv, pq, pk, pv, w)
+    return pl.pallas_call(
+        publish,
+        out_shape=tuple(jax.ShapeDtypeStruct(r.shape, r.dtype) for r in results),
+        in_specs=[any_space] * 2,
+        out_specs=(any_space,) * 2,
+        scratch_shapes=[vm((BLK, WIDE), BF16), vm((HALF, FEATS), BF16), dma((PARTS + 1,)), dma((PARTS + 1,))],
+        compiler_params=pltpu.CompilerParams(vmem_limit_bytes=56 * 2**20),
+        name="publish",
+    )(*results)
 
 
 def solution(mesh):

time: 63.4 us -> 59.8 us (0.943)
  local copies, waits for them, and re-layouts: 3.29 us -> 0 us
    unnamed x4 -> x0, local copies, waits for them, and re-layouts: 3.29 us -> none
    pallas_call x1, Pallas kernels: 59.1 us -> 56.5 us  [on_device(): pl.pallas_call(kernel, out_shape=(jax.ShapeDtypeStruct((BLK, WIDE), BF16)...]
    pallas_call x0 -> x1, Pallas kernels: none -> 2.24 us  [on_device(): pl.pallas_call(publish, out_shape=tuple((jax.ShapeDtypeStruct(r.shape, r....]
where the time goes in v3:
time: 59.8 us; the launch traced here: 59.4 us
  Pallas kernels  58.7 us (98%)
  between operations  0.64 us (1%)
    pallas_call x1, Pallas kernels, on_device(): pl.pallas_call(kernel, out_shape=(jax.ShapeDtypeStruct((BLK, WIDE), BF16)...  56.5 us
    pallas_call x1, Pallas kernels, on_device(): pl.pallas_call(publish, out_shape=tuple((jax.ShapeDtypeStruct(r.shape, r....  2.24 us

profile of v3, /device:TPU:17, one launch (start us, length us, event | category | flops | bytes accessed | tf_op | source)
XLA Modules:
  0.0 59.4 jit_solution(4471887966482189310)
XLA Ops:
  0.6 56.5 %star.1 = (bf16[768,1024]{1,0:T(8,128)(2,1)}, bf16[64,256]{1,0:T(8,128)(2,1)}) custom-call(bf16[768,1024]{1,0:T(8,128)(2,1)} %cq.1, bf16[768,128]{1,0:T(8,128)(2,1)} %ck.1, bf16[768,128]{1,0:T(8,128)(2,1)} %cv.1, bf16[16,1024]{1,0:T(8,128)(2,1)} %pq.1, bf16[16,128]{1,0:T(8,128)(2,1)} %pk.1, bf16[16,128]{1,0:T(8,128)(2,1)} %pv.1, bf16[1024,256]{1,0:T(8,128)(2,1)} %w.1), custom_call_target="tpu_custom_call" | custom-call | flops 12000000000 | bytes 5000000 | tf_op jit(solution)/shard_map/star/pallas_call | solution.py:494
  57.1 2.2 %publish.1 = (bf16[768,1024]{1,0:T(8,128)(2,1)}, bf16[64,256]{1,0:T(8,128)(2,1)}) custom-call(bf16[768,1024]{1,0:T(8,128)(2,1)} %get-tuple-element.4.enc, bf16[64,256]{1,0:T(8,128)(2,1)} %get-tuple-element.5.ans), custom_call_target="tpu_custom_call" | custom-call | tf_op jit(solution)/shard_map/publish/pallas_call | solution.py:524

commit v4 on v3

--- a/solution.py
+++ b/solution.py
@@ -20,7 +20,7 @@
 HELD = BLK + ROWS
 KEYS = BLK + 128
 PIECE = 2 * BLK // NZ
-QUARTER = PIECE // NY
+SHARE = PIECE // 2
 EARLY = 3
 AG_UNITS = 3
 HALF = NZ * ROWS // 2
@@ -100,6 +100,9 @@
         return remote(qz.at[z], qz.at[z], q_ss.at[d], q_rr.at[z], at_z(d))
 
 
+    half_of = y % 2
+    partner = y + 1 - 2 * half_of
+
     def root_send(p):
         if p < NZ // 2:
             src = ck.at[pl.ds(p * PIECE, PIECE)]
@@ -107,14 +110,14 @@
             src = cv.at[pl.ds((p - NZ // 2) * PIECE, PIECE)]
         return remote(src, stage, n_ss.at[p], n_rr.at[0], (p, t))
 
-    def quarter_send(row):
-        return remote(stage.at[pl.ds(row * QUARTER, QUARTER)], anc.at[row, z], n_qs.at[row], n_rr.at[1], at_y(row))
+    def share_send(row):
+        src = stage.at[pl.ds(row % 2 * SHARE, SHARE)]
+        return remote(src, anc.at[row % 2, z], n_qs.at[row], n_rr.at[1], at_y(row))
 
     def anchor_z(d):
-        return remote(anc.at[y, z], anc.at[y, z], n_zs.at[d], n_zr.at[z], at_z(d))
-
-    def anchor_y(row, i):
-        return remote(anc.at[y], anc.at[y], n_ys.at[i], n_yr.at[y], at_y(row))
+        return remote(anc.at[half_of, z], anc.at[half_of, z], n_zs.at[d], n_zr.at[z], at_z(d))
+
+    anchor_y = remote(anc.at[half_of], anc.at[half_of], n_ys, n_yr, at_y(partner))
 
     root_own = pltpu.make_async_copy(ck.at[pl.ds(0, PIECE)], stage, loc.at[7])
 
@@ -128,7 +131,7 @@
     for d in FAR_FIRST:
         q_send(d).start()
 
-    def anchor_quarters():
+    def anchor_shares():
         @pl.when(c == 0)
         def _():
             root_own.wait()
@@ -138,21 +141,20 @@
             arrived(stage, n_rr.at[0])
 
         for row in (2, 1, 3):
-            quarter_send(row).start()
-        anc[0, z] = stage[:QUARTER]
+            share_send(row).start()
+        anc[0, z] = stage[:SHARE]
         for d in FAR_FIRST:
             anchor_z(d).start()
 
     def anchor_along_z():
-        arrived(anc.at[y, z], n_rr.at[1])
+        arrived(anc.at[half_of, z], n_rr.at[1])
         for d in FAR_FIRST:
             anchor_z(d).start()
 
     def anchor_along_y():
         for d in range(1, NZ):
-            arrived(anc.at[y, (z + d) % NZ], n_zr.at[(z + d) % NZ])
-        for i, row in enumerate((far, up, down)):
-            anchor_y(row, i).start()
+            arrived(anc.at[half_of, (z + d) % NZ], n_zr.at[(z + d) % NZ])
+        anchor_y.start()
 
     def keys_of(row):
         return kall.at[row, pl.ds(0, HELD)]
@@ -228,7 +230,7 @@
 
     @pl.when(y == 0)
     def _():
-        anchor_quarters()
+        anchor_shares()
 
     w_send(0, y, up, 0).start()
     w_send(1, y, down, 1).start()
@@ -249,33 +251,35 @@
     STACK = HEADS * ROWS
 
     def prompt(i, carry):
-        halves = (i // 3, jnp.where((i == 0) | (i > 1), 1, 0))
-        steps = (jnp.where(i == 0, 0, jnp.where(i == 1, 3, jnp.where(i == 2, 2, 1))),
-                 jnp.where(i == 0, 0, jnp.where(i == 1, 1, jnp.where(i == 2, 3, 2))))
+        halves = (0, 1)
+        steps = (jnp.where(i == 0, 0, jnp.where(i == 1, 3, i - 1)),) * 2
 
         @pl.when(i == 1)
         def _():
             arrived(values_of(down), v_rr.at[down])
+            spread_values(down)
+
+        @pl.when(i == 2)
+        def _():
             arrived(keys_of(up), k_rr.at[up])
             kt[up] = kall[up].T
-            spread_values(down)
             spread_values(up)
 
-        @pl.when(i == 2)
+        @pl.when(i == 3)
         def _():
             arrived(keys_of(far), k_rr.at[far])
             arrived(values_of(far), v_rr.at[far])
             kt[far] = kall[far].T
             spread_values(far)
 
-        @pl.when((i == 2) & (y != 0))
+        @pl.when((i == 3) & (y != 0))
         def _():
             anchor_along_z()
 
         r = lax.broadcasted_iota(jnp.int32, (STACK, 128), 0) % ROWS
         k = lax.broadcasted_iota(jnp.int32, (STACK, 128), 1)
         pairs = [
-            (a, (y + step) % NY, pl.ds(pl.multiple_of(a * (QUAD * STACK), QUAD * STACK), QUAD * STACK))
+            (a, (y + step) % NY, pl.ds(a * (QUAD * STACK), QUAD * STACK))
             for a, step in zip(halves, steps)
         ]
         scores = []
@@ -297,11 +301,6 @@
             po[rows, :HEAD] = po[rows, :HEAD] * f_old + o[:, :HEAD] * f
             po[rows, HEAD:] = po[rows, HEAD:] * f_old + o[:, HEAD:] * f
 
-        @pl.when(i >= 2)
-        def _():
-            for g in range(QUAD):
-                send_partial((i - 2) * QUAD + g)
-
         return carry
 
     lane = lax.broadcasted_iota(jnp.int32, (ROWS, 128), 1)
@@ -312,7 +311,7 @@
     def send_partial(j):
         stats = jnp.zeros((ROWS, 128), F32)
         for h in range(HEADS):
-            rows = pl.ds(pl.multiple_of((j * HEADS + h) * ROWS, ROWS), ROWS)
+            rows = slice((j * HEADS + h) * ROWS, (j * HEADS + h + 1) * ROWS)
             m = pm[rows]
             even = jnp.ceil(m * 0.25) * 4
             f = jnp.exp2(m - even)
@@ -324,13 +323,14 @@
             stats = jnp.where(lane == 16 + h, even, stats)
         r3s[j, :, WIDE:] = stats.astype(BF16)
 
-        @pl.when(j != 6)
-        def _():
+        if j != 6:
             r3_send(j).start()
 
-    lax.fori_loop(0, 4, prompt, 0)
+    lax.fori_loop(0, NY, prompt, 0)
+    for j in (2, 1, 3, 0, 4, 7, 5, 6):
+        send_partial(j)
+    lax.fori_loop(EARLY, HEADS // 2, loop_a, 0)
     anchor_along_y()
-    lax.fori_loop(EARLY, HEADS // 2, loop_a, 0)
 
     seen = jnp.where(c > 0, 0.0, NEG)
 
@@ -347,6 +347,11 @@
         below = om[h, :, HEAD : 2 * HEAD] * f_own + o[:, HEAD:] * f
         out_v[:, cols] = (above / below).astype(BF16)
         return carry
+
+    w_wait(0, down)
+    w_send(0, down, up, 2).start()
+    w_wait(1, up)
+    w_send(1, up, down, 2).start()
 
     for j in range(NZ):
         if j != 6:
@@ -371,15 +376,9 @@
     for d in FAR_FIRST:
         a_send(d).start()
 
-    w_wait(0, down)
-    w_send(0, down, up, 2).start()
-    w_wait(1, up)
-    w_send(1, up, down, 2).start()
-
-    for row in (up, down, far):
-        arrived(anc.at[row], n_yr.at[row])
-    for i in range(NY):
-        at = slice(PIECE * i, PIECE * (i + 1))
+    arrived(anc.at[1 - half_of], n_yr)
+    for i in range(2):
+        at = slice(BLK // 2 * i, BLK // 2 * (i + 1))
         kta[:, at] = jnp.concatenate([anc[i, p] for p in range(NZ // 2)], axis=0).T
         vaa[at, :HEAD] = jnp.concatenate([anc[i, NZ // 2 + p] for p in range(NZ // 2)], axis=0)
 
@@ -446,10 +445,9 @@
     @pl.when(y == 0)
     def _():
         for row in (2, 1, 3):
-            quarter_send(row).wait_send()
-
-    for i, row in enumerate((far, up, down)):
-        anchor_y(row, i).wait_send()
+            share_send(row).wait_send()
+
+    anchor_y.wait_send()
 
     for i, row in enumerate((y, y, down)):
         k_send(row, up, i).wait_send()
@@ -506,13 +504,13 @@
             vm((HEADS, BLK, 3 * HEAD), F32), vm((BLK, WIDE), BF16),
             vm((NZ, ROWS, WIDE), BF16), vm((NZ * HEADS * ROWS, HEAD), BF16),
             vm((NZ * HEADS * ROWS, 2 * HEAD), F32), vm((NZ * HEADS * ROWS, HEAD), F32),
-            vm((NZ, ROWS, WIDE), BF16), vm((PIECE, HEAD), BF16), vm((NY, NZ, QUARTER, HEAD), BF16),
+            vm((NZ, ROWS, WIDE), BF16), vm((PIECE, HEAD), BF16), vm((2, NZ, SHARE, HEAD), BF16),
             vm((NZ, ROWS, MSG), BF16), vm((NZ, ROWS, MSG), BF16),
             vm((2, HALF, NY * FEATS), F32), vm((HALF, NY * FEATS), F32),
             vm((NY, HALF, FEATS), BF16), vm((NX, HALF, FEATS), BF16),
             dma((10,)), dma((NZ,)), dma((NZ,)), dma((3,)), dma((NY,)), dma((3,)), dma((NY,)),
             dma((2, 3)), dma((2, NY)),
-            dma((NZ,)), dma((NY,)), dma((NZ,)), dma((3,)), dma((2,)), dma((NZ,)), dma((NY,)), dma((NZ,)), dma((NZ,)),
+            dma((NZ,)), dma((NY,)), dma((NZ,)), dma, dma((2,)), dma((NZ,)), dma, dma((NZ,)), dma((NZ,)),
             dma((NZ,)), dma((NZ,)), dma, dma, dma((NY,)), dma((NX,)),
         ],
         compiler_params=pltpu.CompilerParams(

time: 59.8 us -> 58.3 us (0.975)
  Pallas kernels: 58.7 us -> 57.2 us
    pallas_call x1, Pallas kernels: 56.5 us -> 55 us  [on_device(): pl.pallas_call(kernel, out_shape=(jax.ShapeDtypeStruct((BLK, WIDE), BF16)...]
where the time goes in v4:
time: 58.3 us; the launch traced here: 57.9 us
  Pallas kernels  57.2 us (98%)
  between operations  0.64 us (1%)
    pallas_call x1, Pallas kernels, on_device(): pl.pallas_call(kernel, out_shape=(jax.ShapeDtypeStruct((BLK, WIDE), BF16)...  55 us
    pallas_call x1, Pallas kernels, on_device(): pl.pallas_call(publish, out_shape=tuple((jax.ShapeDtypeStruct(r.shape, r....  2.24 us

profile of v4, /device:TPU:17, one launch (start us, length us, event | category | flops | bytes accessed | tf_op | source)
XLA Modules:
  0.0 57.9 jit_solution(2376715233132851746)
XLA Ops:
  0.6 55.0 %star.1 = (bf16[768,1024]{1,0:T(8,128)(2,1)}, bf16[64,256]{1,0:T(8,128)(2,1)}) custom-call(bf16[768,1024]{1,0:T(8,128)(2,1)} %cq.1, bf16[768,128]{1,0:T(8,128)(2,1)} %ck.1, bf16[768,128]{1,0:T(8,128)(2,1)} %cv.1, bf16[16,1024]{1,0:T(8,128)(2,1)} %pq.1, bf16[16,128]{1,0:T(8,128)(2,1)} %pk.1, bf16[16,128]{1,0:T(8,128)(2,1)} %pv.1, bf16[1024,256]{1,0:T(8,128)(2,1)} %w.1), custom_call_target="tpu_custom_call" | custom-call | flops 12000000000 | bytes 5000000 | tf_op jit(solution)/shard_map/star/pallas_call | solution.py:492
  55.6 2.2 %publish.1 = (bf16[768,1024]{1,0:T(8,128)(2,1)}, bf16[64,256]{1,0:T(8,128)(2,1)}) custom-call(bf16[768,1024]{1,0:T(8,128)(2,1)} %get-tuple-element.4.enc, bf16[64,256]{1,0:T(8,128)(2,1)} %get-tuple-element.5.ans), custom_call_target="tpu_custom_call" | custom-call | tf_op jit(solution)/shard_map/publish/pallas_call | solution.py:522

commit v5 on v4

--- a/solution.py
+++ b/solution.py
@@ -389,38 +389,43 @@
     ]
     enc_out[0].start()
 
-    for part in range(2):
-        if part == 0:
-            w_wait(0, up)
-            w_wait(1, down)
-        w_wait(part, far)
+    w_wait(0, up)
+    w_wait(1, down)
     for d in range(1, NZ):
         arrived(att.at[(z + d) % NZ], a_rr.at[(z + d) % NZ])
     rows = jnp.concatenate([att[i] for i in range(NZ)], axis=0)
-    for b in range(NY):
-        part = dot(rows, wall[b])
-        for i in range(2):
-            pacc[i, :, FEATS * b : FEATS * (b + 1)] = part[HALF * i : HALF * (i + 1)]
-
-    c_send = remote(pacc.at[1 - core], pgot, c_ss, c_rr, (c, x * NK + 1 - core))
-    c_send.start()
-    c_send.wait_recv()
+
+    owners = (y, up, down, far)
+
+    def c_send(i):
+        return remote(pacc.at[1 - core, i], pgot.at[i], c_ss.at[i], c_rr.at[i], (c, x * NK + 1 - core))
+
+    for i, row in enumerate(owners):
+        if i == 3:
+            w_wait(0, far)
+            w_wait(1, far)
+        part = dot(rows, wall[row])
+        for half in range(2):
+            pacc[half, i] = part[HALF * half : HALF * (half + 1)]
+        c_send(i).start()
 
     def f_send(row):
         return remote(fsend.at[row], fgot.at[x], f_ss.at[row], f_rr.at[x], (row * NZ + z, y * NK + core))
 
-    for row in range(NY):
-        cols = slice(FEATS * row, FEATS * (row + 1))
-        piece = pacc[core, :, cols] + pgot[:, cols]
-        home = (x == y) & (y == row)
-
-        @pl.when(home)
-        def _(piece=piece):
-            fgot[x] = piece.astype(BF16)
-
-        @pl.when(jnp.logical_not(home))
-        def _(piece=piece, row=row):
-            fsend[row] = piece.astype(BF16)
+    for i, row in enumerate(owners):
+        c_send(i).wait_recv()
+        piece = (pacc[core, i] + pgot[i]).astype(BF16)
+        if i == 0:
+            @pl.when(x == y)
+            def _(piece=piece):
+                fgot[x] = piece
+
+            @pl.when(x != y)
+            def _(piece=piece):
+                fsend[y] = piece
+                f_send(y).start()
+        else:
+            fsend[row] = piece
             f_send(row).start()
 
     lax.fori_loop(AG_UNITS, HEADS, anchor_unit, 0)
@@ -457,7 +462,8 @@
     for j in range(NZ):
         if j != 6:
             r3_send(j).wait_send()
-    c_send.wait_send()
+    for i in range(NY):
+        c_send(i).wait_send()
     for row in range(NY):
         @pl.when((x != y) | (y != row))
         def _(row=row):
@@ -506,12 +512,12 @@
             vm((NZ * HEADS * ROWS, 2 * HEAD), F32), vm((NZ * HEADS * ROWS, HEAD), F32),
             vm((NZ, ROWS, WIDE), BF16), vm((PIECE, HEAD), BF16), vm((2, NZ, SHARE, HEAD), BF16),
             vm((NZ, ROWS, MSG), BF16), vm((NZ, ROWS, MSG), BF16),
-            vm((2, HALF, NY * FEATS), F32), vm((HALF, NY * FEATS), F32),
+            vm((2, NY, HALF, FEATS), F32), vm((NY, HALF, FEATS), F32),
             vm((NY, HALF, FEATS), BF16), vm((NX, HALF, FEATS), BF16),
             dma((10,)), dma((NZ,)), dma((NZ,)), dma((3,)), dma((NY,)), dma((3,)), dma((NY,)),
             dma((2, 3)), dma((2, NY)),
             dma((NZ,)), dma((NY,)), dma((NZ,)), dma, dma((2,)), dma((NZ,)), dma, dma((NZ,)), dma((NZ,)),
-            dma((NZ,)), dma((NZ,)), dma, dma, dma((NY,)), dma((NX,)),
+            dma((NZ,)), dma((NZ,)), dma((NY,)), dma((NY,)), dma((NY,)), dma((NX,)),
         ],
         compiler_params=pltpu.CompilerParams(
             collective_id=0, has_side_effects=True, vmem_limit_bytes=56 * 2**20

time: 58.3 us -> 58.7 us (level)
  no operation moved by 1% of the time
where the time goes in v5:
time: 58.7 us; the launch traced here: 57.8 us
  Pallas kernels  57.1 us (97%)
  between operations  0.64 us (1%)
    pallas_call x1, Pallas kernels, on_device(): pl.pallas_call(kernel, out_shape=(jax.ShapeDtypeStruct((BLK, WIDE), BF16)...  54.9 us
    pallas_call x1, Pallas kernels, on_device(): pl.pallas_call(publish, out_shape=tuple((jax.ShapeDtypeStruct(r.shape, r....  2.24 us

profile of v5, /device:TPU:17, one launch (start us, length us, event | category | flops | bytes accessed | tf_op | source)
XLA Modules:
  0.0 57.8 jit_solution(8697338835131839341)
XLA Ops:
  0.6 54.9 %star.1 = (bf16[768,1024]{1,0:T(8,128)(2,1)}, bf16[64,256]{1,0:T(8,128)(2,1)}) custom-call(bf16[768,1024]{1,0:T(8,128)(2,1)} %cq.1, bf16[768,128]{1,0:T(8,128)(2,1)} %ck.1, bf16[768,128]{1,0:T(8,128)(2,1)} %cv.1, bf16[16,1024]{1,0:T(8,128)(2,1)} %pq.1, bf16[16,128]{1,0:T(8,128)(2,1)} %pk.1, bf16[16,128]{1,0:T(8,128)(2,1)} %pv.1, bf16[1024,256]{1,0:T(8,128)(2,1)} %w.1), custom_call_target="tpu_custom_call" | custom-call | flops 12000000000 | bytes 5000000 | tf_op jit(solution)/shard_map/star/pallas_call | solution.py:498
  55.5 2.2 %publish.1 = (bf16[768,1024]{1,0:T(8,128)(2,1)}, bf16[64,256]{1,0:T(8,128)(2,1)}) custom-call(bf16[768,1024]{1,0:T(8,128)(2,1)} %get-tuple-element.4.enc, bf16[64,256]{1,0:T(8,128)(2,1)} %get-tuple-element.5.ans), custom_call_target="tpu_custom_call" | custom-call | tf_op jit(solution)/shard_map/publish/pallas_call | solution.py:528
